TPU v7x, 32 devices: a whole 2x2x4 slice. The times are simulated.
32 devices in a mesh: fsdp: 8 (over y, x, core), tensor: 4 (over z).
Axes of the slice: x: 2, y: 2, z: 4, core: 2. Of those that a mesh axis runs over, the one named last changes fastest.
Arguments:
- image_rows: bfloat16 [16, 1024, 1024], P('fsdp', 'tensor'), may hold values from -6 to 6
- text_rows: bfloat16 [16, 128, 1024], P('fsdp', 'tensor'), may hold values from -6 to 6
- segment_ids: int32 [16, 128], P('fsdp'), may hold values from 0 to 3, as said below
- cotangent: bfloat16 [16, 1024, 1024], P('fsdp', 'tensor'), may hold values from -6 to 6
- query_weight: bfloat16 [1024, 1024], P('fsdp', 'tensor'), may hold values from -0.1875 to 0.1875
- key_weight: bfloat16 [1024, 1024], P('fsdp', 'tensor'), may hold values from -0.1875 to 0.1875
- value_weight: bfloat16 [1024, 1024], P('fsdp', 'tensor'), may hold values from -0.1875 to 0.1875
- attn_output: bfloat16 [1024, 1024], P('fsdp', 'tensor'), may hold values from -1.5 to 1.5
- cross_query: bfloat16 [1024, 1024], P('fsdp', 'tensor'), may hold values from -0.1875 to 0.1875
- cross_key: bfloat16 [1024, 1024], P('fsdp', 'tensor'), may hold values from -0.1875 to 0.1875
- cross_value: bfloat16 [1024, 1024], P('fsdp', 'tensor'), may hold values from -0.1875 to 0.1875
- cross_output: bfloat16 [1024, 1024], P('fsdp', 'tensor'), may hold values from -0.75 to 0.75
- hidden_in: bfloat16 [1024, 4096], P('fsdp', 'tensor'), may hold values from -0.1875 to 0.1875
- hidden_out: bfloat16 [1024, 4096], P('fsdp', 'tensor'), may hold values from -0.09375 to 0.09375
- gain_attn: float32 [1024], P('fsdp'), may hold values from 0.25 to 1.75
- bias_attn: float32 [1024], P('fsdp'), may hold values from -4 to 4
- gain_cross: float32 [1024], P('fsdp'), may hold values from 0.25 to 1.75
- bias_cross: float32 [1024], P('fsdp'), may hold values from -4 to 4
- gain_mlp: float32 [1024], P('fsdp'), may hold values from 0.25 to 1.75
- bias_mlp: float32 [1024], P('fsdp'), may hold values from -4 to 4
Outputs:
- result: bfloat16 [16, 1024, 1024], P('fsdp', 'tensor')
- input_grad: float32 [16, 1024, 1024], P('fsdp', 'tensor')
- text_grad: float32 [16, 128, 1024], P('fsdp', 'tensor')
- grad_query_weight: float32 [1024, 1024], P('fsdp', 'tensor')
- grad_key_weight: float32 [1024, 1024], P('fsdp', 'tensor')
- grad_value_weight: float32 [1024, 1024], P('fsdp', 'tensor')
- grad_attn_output: float32 [1024, 1024], P('fsdp', 'tensor')
- grad_cross_query: float32 [1024, 1024], P('fsdp', 'tensor')
- grad_cross_key: float32 [1024, 1024], P('fsdp', 'tensor')
- grad_cross_value: float32 [1024, 1024], P('fsdp', 'tensor')
- grad_cross_output: float32 [1024, 1024], P('fsdp', 'tensor')
- grad_hidden_in: float32 [1024, 4096], P('fsdp', 'tensor')
- grad_hidden_out: float32 [1024, 4096], P('fsdp', 'tensor')
- grad_gain_attn: float32 [1024], P('fsdp')
- grad_bias_attn: float32 [1024], P('fsdp')
- grad_gain_cross: float32 [1024], P('fsdp')
- grad_bias_cross: float32 [1024], P('fsdp')
- grad_gain_mlp: float32 [1024], P('fsdp')
- grad_bias_mlp: float32 [1024], P('fsdp')
Inputs may be any that keep to these rules, and one draw needn't show every extreme that they name: `segment_ids`: along each row the ids never fall, and each of the 4 ids appears.
All inputs are finite; a program needn't handle non-finite values.
Results may differ from a plain program's by a relative error of at most 0.035.
Values may be sent and summed in bfloat16 or wider, within the bound.
No kernel may reach another device: no remote copies, remote signals or barrier semaphores. Data moves between devices by JAX's collectives and lax.ppermute only.
A program may use at most 192 MiB of HBM per device.

v0:
```python
import math

import jax
import jax.numpy as jnp
from jax import lax
from jax.sharding import PartitionSpec as P

HD = 64
SEQ = 1024
TXT = 128


EPS = 1e-05
NEG = -1e30


def layer_norm(values, gain, offset):
    center = values - jnp.mean(values, -1, keepdims=True)
    spread = jnp.mean(center * center, -1, keepdims=True)
    return center * lax.rsqrt(spread + EPS) * gain + offset


def gelu_tanh(values):
    return (
        0.5
        * values
        * (
            1.0
            + jnp.tanh(math.sqrt(2.0 / math.pi) * (values + 0.044715 * values * values * values))
        )
    )


def norm_back(values, gain, offset, grad_normed):
    unused_out, pullback = jax.vjp(layer_norm, values, gain, offset)
    return pullback(grad_normed)


def project(rows_in, weight):
    return jnp.einsum("bsd,de->bse", rows_in, weight, preferred_element_type=jnp.float32)


def back_project(grads_in, weight):
    return jnp.einsum("bse,de->bsd", grads_in, weight, preferred_element_type=jnp.float32)


def weight_grad(rows_in, grads_in):
    return jnp.einsum("bsd,bse->de", rows_in, grads_in, preferred_element_type=jnp.float32)


def head_view(rows_in):
    return rows_in.reshape(rows_in.shape[0], -1, HD)


def allowed(causal, row_start, row_count, segs_row, key_count):
    row_ids = row_start + lax.iota(jnp.int32, row_count)[:, None]
    col_ids = lax.iota(jnp.int32, key_count)[None, :]
    if causal:
        return col_ids <= row_ids
    text_place = row_ids * TXT // SEQ
    caption = jnp.sum(jnp.where(col_ids == text_place, segs_row[None, :], 0), -1, keepdims=True)
    return segs_row[None, :] == caption


def block_scores(query_block, key_heads, row_start, segs_row, causal):
    scores = jnp.einsum(
        "qhd,khd->hqk", query_block, key_heads, preferred_element_type=jnp.float32
    ) * HD ** (-0.5)
    visible = allowed(causal, row_start, query_block.shape[0], segs_row, key_heads.shape[0])
    return jnp.where(visible[None], scores, NEG)


def attend_image(query_heads, key_heads, value_heads, segs_row, causal):
    length = query_heads.shape[0]
    block_rows = min(512, length)
    block_count = length // block_rows
    head_count = query_heads.shape[1]
    grouped = query_heads.reshape(block_count, block_rows, head_count, HD)

    def one_block(packed_in):
        query_block, block_index = packed_in
        scores = block_scores(query_block, key_heads, block_index * block_rows, segs_row, causal)
        peak_score = jnp.max(scores, -1, keepdims=True)
        weights = jnp.exp(scores - peak_score)
        norm_total = jnp.sum(weights, -1, keepdims=True)
        prob_low = (weights / norm_total).astype(jnp.bfloat16)
        block_mix = jnp.einsum(
            "hqk,khd->qhd", prob_low, value_heads, preferred_element_type=jnp.float32
        )
        return (block_mix, (peak_score + jnp.log(norm_total))[..., 0])

    block_mix, logsum = lax.map(one_block, (grouped, jnp.arange(block_count, dtype=jnp.int32)))
    return (block_mix.reshape(length, head_count * HD), logsum)


def attend_back(query_heads, key_heads, value_heads, logsum, grad_heads, segs_row, causal):
    length = query_heads.shape[0]
    block_rows = min(512, length)
    block_count = length // block_rows
    head_count = query_heads.shape[1]
    grouped = query_heads.reshape(block_count, block_rows, head_count, HD)
    grad_grouped = grad_heads.reshape(block_count, block_rows, head_count, HD)
    scale_value = HD ** (-0.5)

    def one_block(carry, packed_in):
        key_grad, value_grad = carry
        query_block, grad_block, block_sum, block_index = packed_in
        scores = block_scores(query_block, key_heads, block_index * block_rows, segs_row, causal)
        weights = jnp.exp(scores - block_sum[..., None])
        weight_low = weights.astype(jnp.bfloat16)
        value_grad = value_grad + jnp.einsum(
            "hqk,qhd->khd", weight_low, grad_block, preferred_element_type=jnp.float32
        )
        prob_grad = jnp.einsum(
            "qhd,khd->hqk", grad_block, value_heads, preferred_element_type=jnp.float32
        )
        row_dot = jnp.sum(weights * prob_grad, -1, keepdims=True)
        score_grad = (weights * (prob_grad - row_dot)).astype(jnp.bfloat16)
        query_grad = (
            jnp.einsum("hqk,khd->qhd", score_grad, key_heads, preferred_element_type=jnp.float32)
            * scale_value
        )
        key_grad = (
            key_grad
            + jnp.einsum(
                "hqk,qhd->khd", score_grad, query_block, preferred_element_type=jnp.float32
            )
            * scale_value
        )
        return ((key_grad, value_grad), query_grad)

    zeros = jnp.zeros(key_heads.shape, jnp.float32)
    (key_grad, value_grad), query_grad = lax.scan(
        one_block,
        (zeros, zeros),
        (grouped, grad_grouped, logsum, jnp.arange(block_count, dtype=jnp.int32)),
    )
    key_count = key_heads.shape[0]
    return (
        query_grad.reshape(length, head_count * HD),
        key_grad.reshape(key_count, head_count * HD),
        value_grad.reshape(key_count, head_count * HD),
    )


def attn_forward(query_rows, source_rows, w_query, w_key, w_value, segment_ids, causal):
    queries = project(query_rows, w_query).astype(jnp.bfloat16)
    key_rows = project(source_rows, w_key).astype(jnp.bfloat16)
    value_rows = project(source_rows, w_value).astype(jnp.bfloat16)

    def attn_per_image(packed_in):
        return attend_image(
            head_view(packed_in[0]),
            head_view(packed_in[1]),
            head_view(packed_in[2]),
            packed_in[3],
            causal,
        )

    mixed_rows, logsum = lax.map(attn_per_image, (queries, key_rows, value_rows, segment_ids))
    return (queries, key_rows, value_rows, mixed_rows.astype(jnp.bfloat16), logsum)


def attention_back(
    query_rows, source_rows, state, grad_full, w_query, w_key, w_value, w_out, segment_ids, causal
):
    queries, key_rows, value_rows, mixed_rows, logsum = state
    mixed_grad = project(grad_full, w_out).astype(jnp.bfloat16)
    out_wgrad = weight_grad(grad_full, mixed_rows)

    def attention_per_image(packed_in):
        return attend_back(
            head_view(packed_in[0]),
            head_view(packed_in[1]),
            head_view(packed_in[2]),
            packed_in[3],
            head_view(packed_in[4]),
            packed_in[5],
            causal,
        )

    query_grad, key_grad, value_grad = lax.map(
        attention_per_image, (queries, key_rows, value_rows, logsum, mixed_grad, segment_ids)
    )
    query_grad = query_grad.astype(jnp.bfloat16)
    key_grad = key_grad.astype(jnp.bfloat16)
    value_grad = value_grad.astype(jnp.bfloat16)
    query_wgrad = weight_grad(query_rows, query_grad)
    key_wgrad = weight_grad(source_rows, key_grad)
    value_wgrad = weight_grad(source_rows, value_grad)
    query_part = back_project(query_grad, w_query)
    source_part = back_project(key_grad, w_key) + back_project(value_grad, w_value)
    return (query_part, source_part, query_wgrad, key_wgrad, value_wgrad, out_wgrad)


def fetch_weights(local_params):
    (
        query_weight,
        key_weight,
        value_weight,
        attn_output,
        cross_query,
        cross_key,
        cross_value,
        cross_output,
        hidden_in,
        hidden_out,
        gain_attn,
        bias_attn,
        gain_cross,
        bias_cross,
        gain_mlp,
        bias_mlp,
    ) = local_params
    return (
        lax.all_gather(query_weight, "fsdp", axis=0, tiled=True),
        lax.all_gather(key_weight, "fsdp", axis=0, tiled=True),
        lax.all_gather(value_weight, "fsdp", axis=0, tiled=True),
        lax.all_gather(attn_output, "fsdp", axis=0, tiled=True),
        lax.all_gather(cross_query, "fsdp", axis=0, tiled=True),
        lax.all_gather(cross_key, "fsdp", axis=0, tiled=True),
        lax.all_gather(cross_value, "fsdp", axis=0, tiled=True),
        lax.all_gather(cross_output, "fsdp", axis=0, tiled=True),
        lax.all_gather(hidden_in, "fsdp", axis=0, tiled=True),
        lax.all_gather(hidden_out, "fsdp", axis=0, tiled=True),
        lax.all_gather(gain_attn.astype(jnp.bfloat16), "fsdp", axis=0, tiled=True).astype(
            gain_attn.dtype
        ),
        lax.all_gather(bias_attn.astype(jnp.bfloat16), "fsdp", axis=0, tiled=True).astype(
            bias_attn.dtype
        ),
        lax.all_gather(gain_cross.astype(jnp.bfloat16), "fsdp", axis=0, tiled=True).astype(
            gain_cross.dtype
        ),
        lax.all_gather(bias_cross.astype(jnp.bfloat16), "fsdp", axis=0, tiled=True).astype(
            bias_cross.dtype
        ),
        lax.all_gather(gain_mlp.astype(jnp.bfloat16), "fsdp", axis=0, tiled=True).astype(
            gain_mlp.dtype
        ),
        lax.all_gather(bias_mlp.astype(jnp.bfloat16), "fsdp", axis=0, tiled=True).astype(
            bias_mlp.dtype
        ),
    )


def spread_rows(rows_in):
    return lax.all_gather(rows_in, "tensor", axis=1, tiled=True)


def spread_grads(grads_in):
    return lax.all_gather(grads_in, "tensor", axis=1, tiled=True)


def branch_sum(partial_sum):
    return lax.psum_scatter(
        partial_sum.astype(jnp.bfloat16), "tensor", scatter_dimension=1, tiled=True
    ).astype(jnp.float32)


def grad_sum(partial_sum):
    return lax.psum_scatter(
        partial_sum.astype(jnp.bfloat16), "tensor", scatter_dimension=1, tiled=True
    ).astype(jnp.float32)


def gather_text(text_rows):
    return lax.all_gather(text_rows, "tensor", axis=1, tiled=True)


def body(
    image_rows,
    text_rows,
    segment_ids,
    cotangent,
    query_weight,
    key_weight,
    value_weight,
    attn_output,
    cross_query,
    cross_key,
    cross_value,
    cross_output,
    hidden_in,
    hidden_out,
    gain_attn,
    bias_attn,
    gain_cross,
    bias_cross,
    gain_mlp,
    bias_mlp,
):
    local_params = (
        query_weight,
        key_weight,
        value_weight,
        attn_output,
        cross_query,
        cross_key,
        cross_value,
        cross_output,
        hidden_in,
        hidden_out,
        gain_attn,
        bias_attn,
        gain_cross,
        bias_cross,
        gain_mlp,
        bias_mlp,
    )
    (
        self_query,
        self_key,
        self_value,
        self_out,
        text_query,
        text_key,
        text_value,
        text_out,
        feed_in,
        feed_out,
        gain_one,
        bias_one,
        gain_two,
        bias_two,
        gain_three,
        bias_three,
    ) = fetch_weights(local_params)
    inputs_wide = image_rows.astype(jnp.float32)
    normed_one = layer_norm(inputs_wide, gain_one, bias_one).astype(jnp.bfloat16)
    full_one = spread_rows(normed_one)
    attn_state = attn_forward(
        full_one, full_one, self_query, self_key, self_value, segment_ids, True
    )
    after_attn = inputs_wide + branch_sum(back_project(attn_state[3], self_out))
    normed_two = layer_norm(after_attn, gain_two, bias_two).astype(jnp.bfloat16)
    full_two = spread_rows(normed_two)
    text_full = gather_text(text_rows)
    cross_state = attn_forward(
        full_two, text_full, text_query, text_key, text_value, segment_ids, False
    )
    after_cross = after_attn + branch_sum(back_project(cross_state[3], text_out))
    normed_three = layer_norm(after_cross, gain_three, bias_three).astype(jnp.bfloat16)
    full_three = spread_rows(normed_three)
    hidden_pre = project(full_three, feed_in)
    hidden_act = gelu_tanh(hidden_pre).astype(jnp.bfloat16)
    result = after_cross + branch_sum(back_project(hidden_act, feed_out))
    grad_top = spread_grads(cotangent)
    act_grad = project(grad_top, feed_out)
    unused_act, gelu_pull = jax.vjp(gelu_tanh, hidden_pre)
    pre_grad = gelu_pull(act_grad)[0].astype(jnp.bfloat16)
    grad_feed_out = weight_grad(grad_top, hidden_act)
    grad_feed_in = weight_grad(full_three, pre_grad)
    normed_three_grad = grad_sum(back_project(pre_grad, feed_in))
    back_three, grad_gain_three, grad_bias_three = norm_back(
        after_cross, gain_three, bias_three, normed_three_grad
    )
    grad_cross = cotangent.astype(jnp.float32) + back_three
    grad_mid = spread_grads(grad_cross.astype(jnp.bfloat16))
    cross_part, text_part, grad_text_query, grad_text_key, grad_text_value, grad_text_out = (
        attention_back(
            full_two,
            text_full,
            cross_state,
            grad_mid,
            text_query,
            text_key,
            text_value,
            text_out,
            segment_ids,
            False,
        )
    )
    normed_two_grad = grad_sum(cross_part)
    text_grad = lax.psum_scatter(
        text_part.astype(jnp.bfloat16), "tensor", scatter_dimension=1, tiled=True
    ).astype(jnp.float32)
    back_two, grad_gain_two, grad_bias_two = norm_back(
        after_attn, gain_two, bias_two, normed_two_grad
    )
    grad_attn = grad_cross + back_two
    grad_low = spread_grads(grad_attn.astype(jnp.bfloat16))
    self_part, source_part, grad_self_query, grad_self_key, grad_self_value, grad_self_out = (
        attention_back(
            full_one,
            full_one,
            attn_state,
            grad_low,
            self_query,
            self_key,
            self_value,
            self_out,
            segment_ids,
            True,
        )
    )
    normed_one_grad = grad_sum(self_part + source_part)
    back_one, grad_gain_one, grad_bias_one = norm_back(
        inputs_wide, gain_one, bias_one, normed_one_grad
    )
    input_grad = grad_attn + back_one
    norm_sums = lax.psum(
        (
            grad_gain_one,
            grad_bias_one,
            grad_gain_two,
            grad_bias_two,
            grad_gain_three,
            grad_bias_three,
        ),
        "tensor",
    )
    summed = (
        lax.psum_scatter(
            grad_self_query.astype(jnp.bfloat16), "fsdp", scatter_dimension=0, tiled=True
        ).astype(jnp.float32),
        lax.psum_scatter(
            grad_self_key.astype(jnp.bfloat16), "fsdp", scatter_dimension=0, tiled=True
        ).astype(jnp.float32),
        lax.psum_scatter(
            grad_self_value.astype(jnp.bfloat16), "fsdp", scatter_dimension=0, tiled=True
        ).astype(jnp.float32),
        lax.psum_scatter(
            grad_self_out.astype(jnp.bfloat16), "fsdp", scatter_dimension=0, tiled=True
        ).astype(jnp.float32),
        lax.psum_scatter(
            grad_text_query.astype(jnp.bfloat16), "fsdp", scatter_dimension=0, tiled=True
        ).astype(jnp.float32),
        lax.psum_scatter(
            grad_text_key.astype(jnp.bfloat16), "fsdp", scatter_dimension=0, tiled=True
        ).astype(jnp.float32),
        lax.psum_scatter(
            grad_text_value.astype(jnp.bfloat16), "fsdp", scatter_dimension=0, tiled=True
        ).astype(jnp.float32),
        lax.psum_scatter(
            grad_text_out.astype(jnp.bfloat16), "fsdp", scatter_dimension=0, tiled=True
        ).astype(jnp.float32),
        lax.psum_scatter(
            grad_feed_in.astype(jnp.bfloat16), "fsdp", scatter_dimension=0, tiled=True
        ).astype(jnp.float32),
        lax.psum_scatter(
            grad_feed_out.astype(jnp.bfloat16), "fsdp", scatter_dimension=0, tiled=True
        ).astype(jnp.float32),
        lax.psum_scatter(
            norm_sums[0].astype(jnp.bfloat16), "fsdp", scatter_dimension=0, tiled=True
        ).astype(jnp.float32),
        lax.psum_scatter(
            norm_sums[1].astype(jnp.bfloat16), "fsdp", scatter_dimension=0, tiled=True
        ).astype(jnp.float32),
        lax.psum_scatter(
            norm_sums[2].astype(jnp.bfloat16), "fsdp", scatter_dimension=0, tiled=True
        ).astype(jnp.float32),
        lax.psum_scatter(
            norm_sums[3].astype(jnp.bfloat16), "fsdp", scatter_dimension=0, tiled=True
        ).astype(jnp.float32),
        lax.psum_scatter(
            norm_sums[4].astype(jnp.bfloat16), "fsdp", scatter_dimension=0, tiled=True
        ).astype(jnp.float32),
        lax.psum_scatter(
            norm_sums[5].astype(jnp.bfloat16), "fsdp", scatter_dimension=0, tiled=True
        ).astype(jnp.float32),
    )
    return (
        result.astype(jnp.bfloat16),
        input_grad,
        text_grad,
        summed[0],
        summed[1],
        summed[2],
        summed[3],
        summed[4],
        summed[5],
        summed[6],
        summed[7],
        summed[8],
        summed[9],
        summed[10],
        summed[11],
        summed[12],
        summed[13],
        summed[14],
        summed[15],
    )


def solution(mesh):
    placed = (
        P("fsdp", "tensor", None),
        P("fsdp", "tensor", None),
        P("fsdp", None),
        P("fsdp", "tensor", None),
        P("fsdp", "tensor"),
        P("fsdp", "tensor"),
        P("fsdp", "tensor"),
        P("fsdp", "tensor"),
        P("fsdp", "tensor"),
        P("fsdp", "tensor"),
        P("fsdp", "tensor"),
        P("fsdp", "tensor"),
        P("fsdp", "tensor"),
        P("fsdp", "tensor"),
        P("fsdp"),
        P("fsdp"),
        P("fsdp"),
        P("fsdp"),
        P("fsdp"),
        P("fsdp"),
    )
    return jax.shard_map(
        body,
        mesh=mesh,
        in_specs=placed,
        out_specs=(
            P("fsdp", "tensor", None),
            P("fsdp", "tensor", None),
            P("fsdp", "tensor", None),
            P("fsdp", "tensor"),
            P("fsdp", "tensor"),
            P("fsdp", "tensor"),
            P("fsdp", "tensor"),
            P("fsdp", "tensor"),
            P("fsdp", "tensor"),
            P("fsdp", "tensor"),
            P("fsdp", "tensor"),
            P("fsdp", "tensor"),
            P("fsdp", "tensor"),
            P("fsdp"),
            P("fsdp"),
            P("fsdp"),
            P("fsdp"),
            P("fsdp"),
            P("fsdp"),
        ),
        check_vma=False,
    )
```

profile of v0, /device:TPU:9, one launch (start us, length us, event | category | flops | bytes accessed | tf_op | source)
XLA Modules:
  0.0 1774.0 jit_solution(10391377912507331138)
XLA Ops:
  72.5 39.4 %all-gather.15.cloned.1.call-done = bf16[2,1024,1024]{2,1,0:T(8,128)(2,1)} async-done(((bf16[2,256,1024]{2,1,0:T(8,128)(2,1)}), bf16[2,1024,1024]{2,1,0:T(8,128)(2,1)}) %all-gather.15.cloned.1.call-update) | async-done | bytes 4194320 | tf_op jit(solution)/shard_map/all_gather | solution.py:248
  126.6 84.4 %while.138 = (s32[]{:T(128)}, bf16[2,1024,256]{1,2,0:T(8,128)(2,1)}, f32[2,2,4,512]{3,2,1,0:T(4,128)S(1)}, bf16[2,1024,256]{1,2,0:T(8,128)(2,1)S(1)}, bf16[2,102...) while((s32[]{:T(128)}, bf16[2,1024,256]{1,2,0:T(8,128)(2,1)}, ...), condition=%wide.region_7.8_spmd, body=%wide.region_2.7_spmd.sunk | while | flops 562559488 | bytes 37327224 | solution.py:160
  128.3 38.1 %while.145 = (s32[]{:T(128)}, bf16[2,512,4,64]{1,0,3,2:T(2,128)(2,1)}, f32[2,4,512]{2,1,0:T(4,128)S(1)}, s32[2]{0:T(128)S(1)}, bf16[2,512,4,64]{1,3,2,0:T(8,128)...) while((s32[]{:T(128)}, ...), condition=%wide.region_6.6_spmd, body=%wide.region_3.5_spmd.sunk | while | flops 562559488 | bytes 29954196 | solution.py:92
  170.5 38.1 %while.145 = (s32[]{:T(128)}, bf16[2,512,4,64]{1,0,3,2:T(2,128)(2,1)}, f32[2,4,512]{2,1,0:T(4,128)S(1)}, s32[2]{0:T(128)S(1)}, bf16[2,512,4,64]{1,3,2,0:T(8,128)...) while((s32[]{:T(128)}, ...), condition=%wide.region_6.6_spmd, body=%wide.region_3.5_spmd.sunk | while | flops 562559488 | bytes 29954196 | solution.py:92
  234.4 59.7 %reduce-scatter.24.cloned.1.call-done = bf16[2,256,1024]{2,1,0:T(8,128)(2,1)} async-done(((bf16[2,1024,1024]{2,1,0:T(8,128)(2,1)}), bf16[2,256,1024]{2,1,0:T(8,128)(2,1)}) %reduce-scatter.24.cloned.1.call-update) | async-done | bytes 1048592 | tf_op jit(solution)/shard_map/reduce_scatter | solution.py:256
  394.7 62.4 %while.140 = (s32[]{:T(128)}, bf16[2,1024,256]{1,2,0:T(8,128)(2,1)}, f32[2,2,4,512]{3,2,1,0:T(4,128)}, bf16[2,1024,256]{1,2,0:T(8,128)(2,1)}, bf16[2,128,256]{1,...) while((s32[]{:T(128)}, bf16[2,1024,256]{1,2,0:T(8,128)(2,1)}, ...), condition=%wide.region_17.18_spmd, body=%wide.region_11.17_spmd.sunk | while | flops 69474304 | bytes 10594710 | solution.py:160
  480.5 59.4 %reduce-scatter.26.cloned.1.call-done = bf16[2,256,1024]{2,1,0:T(8,128)(2,1)} async-done(((bf16[2,1024,1024]{2,1,0:T(8,128)(2,1)}), bf16[2,256,1024]{2,1,0:T(8,128)(2,1)}) %reduce-scatter.26.cloned.1.call-update) | async-done | bytes 1048592 | tf_op jit(solution)/shard_map/reduce_scatter | solution.py:256
  546.1 76.8 %all-gather.19.cloned.1.call-done = bf16[2,1024,1024]{2,1,0:T(8,128)(2,1)} async-done(((bf16[2,256,1024]{2,1,0:T(8,128)(2,1)}), bf16[2,1024,1024]{2,1,0:T(8,128)(2,1)}) %all-gather.19.cloned.1.call-update) | async-done | bytes 4194320 | tf_op jit(solution)/shard_map/all_gather | solution.py:248
  653.9 79.2 %all-gather.25.cloned.1.call-done = bf16[2,1024,1024]{2,1,0:T(8,128)(2,1)} async-done(((bf16[2,256,1024]{2,1,0:T(8,128)(2,1)}), bf16[2,1024,1024]{2,1,0:T(8,128)(2,1)}) %all-gather.25.cloned.1.call-update) | async-done | bytes 4194320 | tf_op jit(solution)/shard_map/all_gather | solution.py:252
  755.5 77.6 %reduce-scatter.30.cloned.1.call-done = bf16[2,256,1024]{2,1,0:T(8,128)(2,1)} async-done(((bf16[2,1024,1024]{2,1,0:T(8,128)(2,1)}), bf16[2,256,1024]{2,1,0:T(8,128)(2,1)}) %reduce-scatter.30.cloned.1.call-update) | async-done | bytes 1048592 | tf_op jit(solution)/shard_map/reduce_scatter | solution.py:262
  841.1 78.6 %all-gather.27.cloned.1.call-done = bf16[2,1024,1024]{2,1,0:T(8,128)(2,1)} async-done(((bf16[2,256,1024]{2,1,0:T(8,128)(2,1)}), bf16[2,1024,1024]{2,1,0:T(8,128)(2,1)}) %all-gather.27.cloned.1.call-update) | async-done | bytes 4194320 | tf_op jit(solution)/shard_map/all_gather | solution.py:252
  925.4 59.8 %while.142 = (s32[]{:T(128)}, bf16[2,1024,256]{1,2,0:T(8,128)(2,1)}, bf16[2,128,256]{1,2,0:T(8,128)(2,1)}, bf16[2,128,256]{1,2,0:T(8,128)(2,1)}, bf16[2,1024,256...) while((s32[]{:T(128)}, bf16[2,1024,256]{1,2,0:T(8,128)(2,1)}, ...), condition=%wide.region_30.31_spmd, body=%wide.region_25.30_spmd.sunk | while | flops 170825728 | bytes 20335104 | solution.py:182
  1001.4 66.6 %reduce-scatter.32.cloned.1.call-done = bf16[2,256,1024]{2,1,0:T(8,128)(2,1)} async-done(((bf16[2,1024,1024]{2,1,0:T(8,128)(2,1)}), bf16[2,256,1024]{2,1,0:T(8,128)(2,1)}) %reduce-scatter.32.cloned.1.call-update) | async-done | bytes 1048592 | tf_op jit(solution)/shard_map/reduce_scatter | solution.py:262
  1074.6 72.9 %reduce-scatter.28.cloned.1.call-done = bf16[2,256,1024]{2,1,0:T(8,128)(2,1)} async-done(((bf16[2,1024,1024]{2,1,0:T(8,128)(2,1)}), bf16[2,256,1024]{2,1,0:T(8,128)(2,1)}) %reduce-scatter.28.cloned.1.call-update) | async-done | bytes 1048592 | tf_op jit(solution)/shard_map/reduce_scatter | solution.py:256
  1188.9 42.3 %all-gather.29.cloned.1.call-done = bf16[2,1024,1024]{2,1,0:T(8,128)(2,1)} async-done(((bf16[2,256,1024]{2,1,0:T(8,128)(2,1)}), bf16[2,1024,1024]{2,1,0:T(8,128)(2,1)}) %all-gather.29.cloned.1.call-update) | async-done | bytes 4194320 | tf_op jit(solution)/shard_map/all_gather | solution.py:252
  1243.4 130.6 %while.144 = (s32[]{:T(128)}, bf16[2,1024,256]{1,2,0:T(8,128)(2,1)}, bf16[2,1024,256]{1,2,0:T(8,128)(2,1)}, bf16[2,1024,256]{1,2,0:T(8,128)(2,1)}, bf16[2,1024,2...) while((s32[]{:T(128)}, bf16[2,1024,256]{1,2,0:T(8,128)(2,1)}, ...), condition=%wide.region_38.39_spmd, body=%wide.region_34.38_spmd.sunk | while | flops 1375730176 | bytes 96301592 | solution.py:182
  1250.0 53.7 %while.148 = (s32[]{:T(128)}, f32[1024,4,64]{0,2,1:T(8,128)S(1)}, f32[1024,4,64]{0,2,1:T(8,128)}, bf16[2,512,4,64]{1,0,3,2:T(2,128)(2,1)}, bf16[2,512,4,64]{1,3,...) while((s32[]{:T(128)}, f32[1024,4,64]{0,2,1:T(8,128)S(1)}, ...), condition=%wide.region_37.37_spmd.clone, body=%wide.region_35.36_spmd.clone.sunk | while | flops 1375730176 | bytes 73199808 | solution.py:133
  1315.2 53.8 %while.148 = (s32[]{:T(128)}, f32[1024,4,64]{0,2,1:T(8,128)S(1)}, f32[1024,4,64]{0,2,1:T(8,128)}, bf16[2,512,4,64]{1,0,3,2:T(2,128)(2,1)}, bf16[2,512,4,64]{1,3,...) while((s32[]{:T(128)}, f32[1024,4,64]{0,2,1:T(8,128)S(1)}, ...), condition=%wide.region_37.37_spmd.clone, body=%wide.region_35.36_spmd.clone.sunk | while | flops 1375730176 | bytes 73199808 | solution.py:133
  1434.4 35.6 %reduce-scatter.46.cloned.1.call-done = bf16[128,256]{1,0:T(8,128)(2,1)} async-done(((bf16[1024,256]{1,0:T(8,128)(2,1)}), bf16[128,256]{1,0:T(8,128)(2,1)}) %reduce-scatter.46.cloned.1.call-update) | async-done | bytes 65552 | tf_op jit(solution)/shard_map/reduce_scatter | solution.py:426
  1492.2 37.7 %reduce-scatter.44.cloned.1.call-done = bf16[128,256]{1,0:T(8,128)(2,1)} async-done(((bf16[1024,256]{1,0:T(8,128)(2,1)}), bf16[128,256]{1,0:T(8,128)(2,1)}) %reduce-scatter.44.cloned.1.call-update) | async-done | bytes 65552 | tf_op jit(solution)/shard_map/reduce_scatter | solution.py:423
  1531.4 35.7 %reduce-scatter.42.cloned.1.call-done = bf16[128,256]{1,0:T(8,128)(2,1)} async-done(((bf16[1024,256]{1,0:T(8,128)(2,1)}), bf16[128,256]{1,0:T(8,128)(2,1)}) %reduce-scatter.42.cloned.1.call-update) | async-done | bytes 65552 | tf_op jit(solution)/shard_map/reduce_scatter | solution.py:420
  1568.6 36.1 %reduce-scatter.38.cloned.1.call-done = bf16[128,256]{1,0:T(8,128)(2,1)} async-done(((bf16[1024,256]{1,0:T(8,128)(2,1)}), bf16[128,256]{1,0:T(8,128)(2,1)}) %reduce-scatter.38.cloned.1.call-update) | async-done | bytes 65552 | tf_op jit(solution)/shard_map/reduce_scatter | solution.py:414
  1606.2 35.7 %reduce-scatter.40.cloned.1.call-done = bf16[128,256]{1,0:T(8,128)(2,1)} async-done(((bf16[1024,256]{1,0:T(8,128)(2,1)}), bf16[128,256]{1,0:T(8,128)(2,1)}) %reduce-scatter.40.cloned.1.call-update) | async-done | bytes 65552 | tf_op jit(solution)/shard_map/reduce_scatter | solution.py:417
  1643.4 78.0 %reduce-scatter.34.cloned.1.call-done = bf16[2,256,1024]{2,1,0:T(8,128)(2,1)} async-done(((bf16[2,1024,1024]{2,1,0:T(8,128)(2,1)}), bf16[2,256,1024]{2,1,0:T(8,128)(2,1)}) %reduce-scatter.34.cloned.1.call-update) | async-done | bytes 1048592 | tf_op jit(solution)/shard_map/reduce_scatter | solution.py:262
  (647 shorter events, 925.8 us)
Async XLA Ops:
  8.1 103.9 %all-gather.15.cloned.1.call-start = ((), (), s32[]{:S(2)}) async-start(), calls=%async_computation.17 | async-start | bytes 5242880 | tf_op jit(solution)/shard_map/all_gather | solution.py:248
  33.8 260.2 %reduce-scatter.24.cloned.1.call-start = ((), (), s32[]{:S(2)}) async-start(), calls=%async_computation.18 | async-start | bytes 5242880 | tf_op jit(solution)/shard_map/reduce_scatter | solution.py:256
  216.1 170.2 %all-gather.17.cloned.1.call-start = ((), (), s32[]{:S(2)}) async-start(), calls=%async_computation.19 | async-start | bytes 5242880 | tf_op jit(solution)/shard_map/all_gather | solution.py:248
  299.1 240.7 %reduce-scatter.26.cloned.1.call-start = ((), (), s32[]{:S(2)}) async-start(), calls=%async_computation.20 | async-start | bytes 5242880 | tf_op jit(solution)/shard_map/reduce_scatter | solution.py:256
  462.4 160.5 %all-gather.19.cloned.1.call-start = ((), (), s32[]{:S(2)}) async-start(), calls=%async_computation.21 | async-start | bytes 5242880 | tf_op jit(solution)/shard_map/all_gather | solution.py:248
  544.3 109.6 %all-gather.23.cloned.1.call-start = ((), (), s32[]{:S(2)}) async-start(), calls=%async_computation.23 | async-start | bytes 2359296 | tf_op jit(solution)/shard_map/all_gather | solution.py:225
  544.9 188.3 %all-gather.25.cloned.1.call-start = ((), (), s32[]{:S(2)}) async-start(), calls=%async_computation.25 | async-start | bytes 5242880 | tf_op jit(solution)/shard_map/all_gather | solution.py:252
  545.6 287.5 %reduce-scatter.30.cloned.1.call-start = ((), (), s32[]{:S(2)}) async-start(), calls=%async_computation.26 | async-start | bytes 5242880 | tf_op jit(solution)/shard_map/reduce_scatter | solution.py:262
  755.2 164.5 %all-gather.27.cloned.1.call-start = ((), (), s32[]{:S(2)}) async-start(), calls=%async_computation.27 | async-start | bytes 5242880 | tf_op jit(solution)/shard_map/all_gather | solution.py:252
  841.0 227.0 %reduce-scatter.32.cloned.1.call-start = ((), (), s32[]{:S(2)}) async-start(), calls=%async_computation.28 | async-start | bytes 5242880 | tf_op jit(solution)/shard_map/reduce_scatter | solution.py:262
  990.0 157.5 %reduce-scatter.28.cloned.1.call-start = ((), (), s32[]{:S(2)}) async-start(), calls=%async_computation.24 | async-start | bytes 5242880 | tf_op jit(solution)/shard_map/reduce_scatter | solution.py:256
  1001.4 229.8 %all-gather.29.cloned.1.call-start = ((), (), s32[]{:S(2)}) async-start(), calls=%async_computation.29 | async-start | bytes 5242880 | tf_op jit(solution)/shard_map/all_gather | solution.py:252
  1152.6 255.6 %reduce-scatter.56.cloned.1.call-start = ((), (), s32[]{:S(2)}) async-start(), calls=%async_computation.41 | async-start | bytes 2359296
  1165.8 244.5 %reduce-scatter.50.cloned.1.call-start = ((), (), s32[]{:S(2)}) async-start(), calls=%async_computation.38 | async-start | bytes 2359296 | tf_op jit(solution)/shard_map/reduce_scatter | solution.py:438
  1175.2 236.8 %reduce-scatter.52.cloned.1.call-start = ((), (), s32[]{:S(2)}) async-start(), calls=%async_computation.39 | async-start | bytes 589824
  1176.7 237.2 %reduce-scatter.54.cloned.1.call-start = ((), (), s32[]{:S(2)}) async-start(), calls=%async_computation.40 | async-start | bytes 589824
  1178.1 254.8 %reduce-scatter.48.cloned.1.call-start = ((), (), s32[]{:S(2)}) async-start(), calls=%async_computation.37 | async-start | bytes 589824 | tf_op jit(solution)/shard_map/reduce_scatter | solution.py:435
  1182.8 287.2 %reduce-scatter.46.cloned.1.call-start = ((), (), s32[]{:S(2)}) async-start(), calls=%async_computation.36 | async-start | bytes 589824 | tf_op jit(solution)/shard_map/reduce_scatter | solution.py:426
  1187.2 303.4 %reduce-scatter.36.cloned.1.call-start = ((), (), s32[]{:S(2)}) async-start(), calls=%async_computation.31 | async-start | bytes 655360 | tf_op jit(solution)/shard_map/reduce_scatter | solution.py:375
  1188.8 341.0 %reduce-scatter.44.cloned.1.call-start = ((), (), s32[]{:S(2)}) async-start(), calls=%async_computation.35 | async-start | bytes 589824 | tf_op jit(solution)/shard_map/reduce_scatter | solution.py:423
  1235.5 331.6 %reduce-scatter.42.cloned.1.call-start = ((), (), s32[]{:S(2)}) async-start(), calls=%async_computation.34 | async-start | bytes 589824 | tf_op jit(solution)/shard_map/reduce_scatter | solution.py:420
  1378.7 226.0 %reduce-scatter.38.cloned.1.call-start = ((), (), s32[]{:S(2)}) async-start(), calls=%async_computation.32 | async-start | bytes 589824 | tf_op jit(solution)/shard_map/reduce_scatter | solution.py:414
  1388.1 253.9 %reduce-scatter.40.cloned.1.call-start = ((), (), s32[]{:S(2)}) async-start(), calls=%async_computation.33 | async-start | bytes 589824 | tf_op jit(solution)/shard_map/reduce_scatter | solution.py:417
  1397.1 324.3 %reduce-scatter.34.cloned.1.call-start = ((), (), s32[]{:S(2)}) async-start(), calls=%async_computation.30 | async-start | bytes 5242880 | tf_op jit(solution)/shard_map/reduce_scatter | solution.py:262
  (88 other events, 6789.0 us)
Sparse Core Ops, SparseCore 0:
  33.9 77.9 all-gather.14
  216.2 77.8 reduce-scatter.23
  299.2 87.0 all-gather.16
  461.9 77.8 reduce-scatter.25
  990.1 77.8 reduce-scatter.31
  1070.2 77.2 reduce-scatter.27
Sparse Core Ops, SparseCore 1:
  464.2 29.2 all-gather.20
  544.4 78.5 all-gather.18
  624.7 29.2 all-gather.22
  655.5 77.6 all-gather.24
  755.3 77.7 reduce-scatter.29
  841.1 78.5 all-gather.26
  1152.7 78.5 all-gather.28
  1234.7 42.0 reduce-scatter.55
  1279.9 41.1 reduce-scatter.49
  1324.5 33.7 reduce-scatter.51
  1361.1 34.1 reduce-scatter.53
  1398.7 34.1 reduce-scatter.47
  1435.8 34.1 reduce-scatter.45
  1472.4 18.2 reduce-scatter.35
  1494.0 35.8 reduce-scatter.43
  1533.0 34.1 reduce-scatter.41
  1570.5 34.1 reduce-scatter.37
  1607.8 34.1 reduce-scatter.39
  1644.2 77.2 reduce-scatter.33
where the time goes:
time: 1800 us; the launch traced here: 1770 us
  waiting for transfers between devices  993 us (55%)
  local copies, waits for them, and re-layouts  246 us (14%)
  matrix products  226 us (13%)
  blocking collectives  189 us (10%)
  other arithmetic  87.7 us (5%)
    reduce_scatter x3, waiting for transfers between devices, grad_sum(): lax.psum_scatter(partial_sum.astype(jnp.bfloat16), 'tensor', scatter_dime...  222 us
    all_gather x3, waiting for transfers between devices, spread_grads(): return lax.all_gather(grads_in, 'tensor', axis=1, tiled=True)  200 us
    reduce_scatter x3, waiting for transfers between devices, branch_sum(): lax.psum_scatter(partial_sum.astype(jnp.bfloat16), 'tensor', scatter_dime...  192 us
    dynamic_update_slice x32, local copies, waits for them, and re-layouts, attend_image(): lax.map(one_block, (grouped, jnp.arange(block_count, dtype=jnp.int32)))  143 us
    all_gather x3, waiting for transfers between devices, spread_rows(): return lax.all_gather(rows_in, 'tensor', axis=1, tiled=True)  139 us
    dot_general x10, matrix products, back_project(): jnp.einsum('bse,de->bsd', grads_in, weight, preferred_element_type=jnp.fl...  51.7 us
    dot_general x10, matrix products, project(): jnp.einsum('bsd,de->bse', rows_in, weight, preferred_element_type=jnp.flo...  48.6 us
    dot_general x10, matrix products, weight_grad(): jnp.einsum('bsd,bse->de', rows_in, grads_in, preferred_element_type=jnp.f...  46.7 us
  transfers between devices with their start and end apart: 25, of which 20 were waited for; matrix products, arithmetic and copies ran while one was open for 14% of the time, Pallas kernels for 0%

commit v1 on v0

v1 whole, which is shorter than its diff:
```python
import functools
import math

import jax
import jax.numpy as jnp
from jax import lax
from jax.experimental import pallas as pl
from jax.experimental.pallas import tpu as pltpu
from jax.sharding import Mesh
from jax.sharding import PartitionSpec as P

HD = 64
EPS = 1e-05
NEG = -1e30
LOG2E = math.log2(math.e)
BF = jnp.bfloat16
F32 = jnp.float32
NT = (((1,), (1,)), ((), ()))
TN = (((0,), (0,)), ((), ()))
NN = (((1,), (0,)), ((), ()))


def dot(left, right, dims=NN):
    return lax.dot_general(left, right, dims, preferred_element_type=F32)


def lane_head(shape, axis, head):
    return lax.broadcasted_iota(jnp.int32, shape, axis) // HD == head


def self_forward_kernel(q_ref, k_ref, v_ref, mix_ref, lse_ref, *, block):
    length = q_ref.shape[0]
    scale = LOG2E * HD**-0.5
    causal = lax.broadcasted_iota(jnp.int32, (block, block), 0) <= lax.broadcasted_iota(
        jnp.int32, (block, block), 1
    )
    for at in range(length // block):
        lo, hi = at * block, (at + 1) * block
        query = q_ref[lo:hi, :]
        mixes = []
        for head in range(2):
            one = jnp.where(lane_head((1, 2 * HD), 1, head), query, jnp.zeros_like(query))
            diag = jnp.where(causal, dot(k_ref[lo:hi, :], one, NT), NEG)
            peak = jnp.max(diag, 0, keepdims=True)
            if at:
                past = dot(k_ref[:lo, :], one, NT)
                peak = jnp.maximum(peak, jnp.max(past, 0, keepdims=True))
            weights = jnp.exp2((diag - peak) * scale)
            total = jnp.sum(weights, 0, keepdims=True)
            mixed = dot(v_ref[lo:hi, :], weights.astype(BF), TN)
            if at:
                weights = jnp.exp2((past - peak) * scale)
                total = total + jnp.sum(weights, 0, keepdims=True)
                mixed = mixed + dot(v_ref[:lo, :], weights.astype(BF), TN)
            mixes.append(mixed / total)
            lse_ref[0, head : head + 1, lo:hi] = peak * scale + jnp.log2(total)
        both = jnp.where(lane_head((2 * HD, 1), 0, 0), mixes[0], mixes[1])
        mix_ref[lo:hi, :] = both.T.astype(BF)


def self_backward_kernel(
    q_ref, k_ref, v_ref, mix_ref, grad_ref, lse_ref, dq_ref, dk_ref, dv_ref, dk_sum, dv_sum, *, block
):
    length = q_ref.shape[0]
    scale = LOG2E * HD**-0.5
    causal = lax.broadcasted_iota(jnp.int32, (block, block), 0) <= lax.broadcasted_iota(
        jnp.int32, (block, block), 1
    )
    dk_sum[...] = jnp.zeros_like(dk_sum)
    dv_sum[...] = jnp.zeros_like(dv_sum)
    for at in range(length // block):
        lo, hi = at * block, (at + 1) * block
        query = q_ref[lo:hi, :]
        grad = grad_ref[lo:hi, :]
        product = (grad.astype(F32) * mix_ref[lo:hi, :].astype(F32)).T
        grads = []
        for head in range(2):
            picked = lane_head((1, 2 * HD), 1, head)
            one = jnp.where(picked, query, jnp.zeros_like(query))
            one_grad = jnp.where(picked, grad, jnp.zeros_like(grad))
            delta = jnp.sum(product[head * HD : (head + 1) * HD], 0, keepdims=True)
            lse = lse_ref[0, head : head + 1, lo:hi]
            total = jnp.zeros((2 * HD, block), F32)
            for start, stop in ((0, lo), (lo, hi)):
                if start == stop:
                    continue
                keys = k_ref[start:stop, :]
                weights = jnp.exp2(dot(keys, one, NT) * scale - lse)
                if start == lo:
                    weights = jnp.where(causal, weights, 0.0)
                slope = dot(v_ref[start:stop, :], one_grad, NT)
                score_grad = (weights * (slope - delta)).astype(BF)
                dv_sum[start:stop, :] += dot(weights.astype(BF), one_grad)
                dk_sum[start:stop, :] += dot(score_grad, one)
                total = total + dot(keys, score_grad, TN)
            grads.append(total)
        both = jnp.where(lane_head((2 * HD, 1), 0, 0), grads[0], grads[1])
        dq_ref[lo:hi, :] = (both.T * HD**-0.5).astype(BF)
    dk_ref[...] = (dk_sum[...] * HD**-0.5).astype(BF)
    dv_ref[...] = dv_sum[...].astype(BF)


def cross_forward_kernel(q_ref, k_ref, v_ref, ids_ref, caption_ref, mix_ref, lse_ref, *, block):
    length = q_ref.shape[0]
    scale = LOG2E * HD**-0.5
    for at in range(length // block):
        lo, hi = at * block, (at + 1) * block
        query = q_ref[lo:hi, :]
        seen = ids_ref[...] == caption_ref[:, lo:hi]
        mixes = []
        for head in range(2):
            one = jnp.where(lane_head((1, 2 * HD), 1, head), query, jnp.zeros_like(query))
            scores = jnp.where(seen, dot(k_ref[...], one, NT), NEG)
            peak = jnp.max(scores, 0, keepdims=True)
            weights = jnp.exp2((scores - peak) * scale)
            total = jnp.sum(weights, 0, keepdims=True)
            mixes.append(dot(v_ref[...], weights.astype(BF), TN) / total)
            lse_ref[0, head : head + 1, lo:hi] = peak * scale + jnp.log2(total)
        both = jnp.where(lane_head((2 * HD, 1), 0, 0), mixes[0], mixes[1])
        mix_ref[lo:hi, :] = both.T.astype(BF)


def cross_backward_kernel(
    q_ref, k_ref, v_ref, mix_ref, grad_ref, lse_ref, ids_ref, caption_ref, dq_ref, dk_ref, dv_ref, *, block
):
    length = q_ref.shape[0]
    scale = LOG2E * HD**-0.5
    keys, values = k_ref[...], v_ref[...]
    dk_sum = jnp.zeros(keys.shape, F32)
    dv_sum = jnp.zeros(keys.shape, F32)
    for at in range(length // block):
        lo, hi = at * block, (at + 1) * block
        query = q_ref[lo:hi, :]
        grad = grad_ref[lo:hi, :]
        product = (grad.astype(F32) * mix_ref[lo:hi, :].astype(F32)).T
        seen = ids_ref[...] == caption_ref[:, lo:hi]
        grads = []
        for head in range(2):
            picked = lane_head((1, 2 * HD), 1, head)
            one = jnp.where(picked, query, jnp.zeros_like(query))
            one_grad = jnp.where(picked, grad, jnp.zeros_like(grad))
            delta = jnp.sum(product[head * HD : (head + 1) * HD], 0, keepdims=True)
            lse = lse_ref[0, head : head + 1, lo:hi]
            weights = jnp.where(seen, jnp.exp2(dot(keys, one, NT) * scale - lse), 0.0)
            slope = dot(values, one_grad, NT)
            score_grad = (weights * (slope - delta)).astype(BF)
            dv_sum = dv_sum + dot(weights.astype(BF), one_grad)
            dk_sum = dk_sum + dot(score_grad, one)
            grads.append(dot(keys, score_grad, TN))
        both = jnp.where(lane_head((2 * HD, 1), 0, 0), grads[0], grads[1])
        dq_ref[lo:hi, :] = (both.T * HD**-0.5).astype(BF)
    dk_ref[...] = (dk_sum * HD**-0.5).astype(BF)
    dv_ref[...] = dv_sum.astype(BF)


def feed_kernel(
    rows_ref, cot_ref, win_ref, wout_ref, out_in, back_in, gin_ref, gout_ref, out_ref, back_ref, rows_t, cot_t, *, first
):
    step = pl.program_id(0)

    @pl.when(step == 0)
    def _():
        rows_t[...] = rows_ref[...].T
        cot_t[...] = cot_ref[...].T
        if first:
            out_ref[...] = jnp.zeros_like(out_ref)
            back_ref[...] = jnp.zeros_like(back_ref)
        else:
            out_ref[...] = out_in[...]
            back_ref[...] = back_in[...]

    pre = dot(rows_ref[...], win_ref[...])
    square = pre * pre
    slope = math.sqrt(2.0 / math.pi)
    bent = jnp.tanh(pre * (slope + slope * 0.044715 * square))
    half = 0.5 * (1.0 + bent)
    act = (pre * half).astype(BF)
    out_ref[...] += dot(act, wout_ref[...], NT)
    gout_ref[...] = dot(cot_t[...], act).astype(BF)
    bend = half + pre * (0.5 * (1.0 - bent * bent)) * (slope + 3.0 * slope * 0.044715 * square)
    pre_grad = (dot(cot_ref[...], wout_ref[...]) * bend).astype(BF)
    gin_ref[...] = dot(rows_t[...], pre_grad).astype(BF)
    back_ref[...] += dot(pre_grad, win_ref[...], NT)


VMEM_LIMIT = 60 * 1024 * 1024


def params():
    return pltpu.CompilerParams(vmem_limit_bytes=VMEM_LIMIT)


def column(rows, offset):
    return pl.BlockSpec((rows, 2 * HD), lambda i: (0, offset + i))


def self_forward(packed):
    length, width = packed.shape
    pairs = width // (6 * HD)
    return pl.pallas_call(
        functools.partial(self_forward_kernel, block=256),
        grid=(pairs,),
        in_specs=[column(length, 0), column(length, pairs), column(length, 2 * pairs)],
        out_specs=[column(length, 0), pl.BlockSpec((1, 2, length), lambda i: (i, 0, 0))],
        out_shape=[
            jax.ShapeDtypeStruct((length, pairs * 2 * HD), BF),
            jax.ShapeDtypeStruct((pairs, 2, length), F32),
        ],
        compiler_params=params(),
        cost_estimate=pl.CostEstimate(
            flops=8 * pairs * length * length * 2 * HD * 2,
            bytes_accessed=8 * pairs * length * 2 * HD,
            transcendentals=2 * pairs * length * length,
        ),
    )(packed, packed, packed)


def self_backward(packed, mix, grad, lse):
    length, width = packed.shape
    pairs = width // (6 * HD)
    part = jax.ShapeDtypeStruct((length, pairs * 2 * HD), BF)
    return pl.pallas_call(
        functools.partial(self_backward_kernel, block=256),
        grid=(pairs,),
        in_specs=[
            column(length, 0),
            column(length, pairs),
            column(length, 2 * pairs),
            column(length, 0),
            column(length, 0),
            pl.BlockSpec((1, 2, length), lambda i: (i, 0, 0)),
        ],
        out_specs=[column(length, 0)] * 3,
        out_shape=[part] * 3,
        scratch_shapes=[pltpu.VMEM((length, 2 * HD), F32)] * 2,
        compiler_params=params(),
        cost_estimate=pl.CostEstimate(
            flops=20 * pairs * length * length * 2 * HD * 2,
            bytes_accessed=16 * pairs * length * 2 * HD,
            transcendentals=2 * pairs * length * length,
        ),
    )(packed, packed, packed, mix, grad, lse)


def cross_forward(queries, keys, ids, captions):
    length, width = queries.shape
    texts = keys.shape[0]
    pairs = width // (2 * HD)
    return pl.pallas_call(
        functools.partial(cross_forward_kernel, block=min(512, length)),
        grid=(pairs,),
        in_specs=[
            column(length, 0),
            column(texts, 0),
            column(texts, pairs),
            pl.BlockSpec((texts, 1), lambda i: (0, 0)),
            pl.BlockSpec((1, length), lambda i: (0, 0)),
        ],
        out_specs=[column(length, 0), pl.BlockSpec((1, 2, length), lambda i: (i, 0, 0))],
        out_shape=[
            jax.ShapeDtypeStruct((length, width), BF),
            jax.ShapeDtypeStruct((pairs, 2, length), F32),
        ],
        compiler_params=params(),
    )(queries, keys, keys, ids, captions)


def cross_backward(queries, keys, mix, grad, lse, ids, captions):
    length, width = queries.shape
    texts = keys.shape[0]
    pairs = width // (2 * HD)
    return pl.pallas_call(
        functools.partial(cross_backward_kernel, block=min(512, length)),
        grid=(pairs,),
        in_specs=[
            column(length, 0),
            column(texts, 0),
            column(texts, pairs),
            column(length, 0),
            column(length, 0),
            pl.BlockSpec((1, 2, length), lambda i: (i, 0, 0)),
            pl.BlockSpec((texts, 1), lambda i: (0, 0)),
            pl.BlockSpec((1, length), lambda i: (0, 0)),
        ],
        out_specs=[column(length, 0), column(texts, 0), column(texts, 0)],
        out_shape=[
            jax.ShapeDtypeStruct((length, width), BF),
            jax.ShapeDtypeStruct((texts, width), BF),
            jax.ShapeDtypeStruct((texts, width), BF),
        ],
        compiler_params=params(),
    )(queries, keys, keys, mix, grad, lse, ids, captions)


def feed(rows, cot, w_in, w_out, sums):
    length, width = rows.shape
    units = w_in.shape[1]
    block = min(256, units)
    whole = pl.BlockSpec((length, width), lambda i: (0, 0))
    cut = pl.BlockSpec((width, block), lambda i: (0, i))
    first = sums is None
    kernel = functools.partial(feed_kernel, first=first)
    operands = [rows, cot, w_in, w_out]
    specs = [whole, whole, cut, cut]
    if first:
        body = lambda a, b, c, d, *rest: kernel(a, b, c, d, None, None, *rest)
    else:
        body = kernel
        operands += list(sums)
        specs += [whole, whole]
    total = jax.ShapeDtypeStruct((length, width), F32)
    part = jax.ShapeDtypeStruct((width, units), BF)
    return pl.pallas_call(
        body,
        grid=(units // block,),
        in_specs=specs,
        out_specs=[cut, cut, whole, whole],
        out_shape=[part, part, total, total],
        scratch_shapes=[pltpu.VMEM((width, length), BF)] * 2,
        compiler_params=params(),
        cost_estimate=pl.CostEstimate(
            flops=12 * length * width * units,
            bytes_accessed=8 * width * units + 8 * length * width,
            transcendentals=length * units,
        ),
    )(*operands)


def norm_parts(values):
    center = values - jnp.mean(values, -1, keepdims=True)
    inverse = lax.rsqrt(jnp.mean(center * center, -1, keepdims=True) + EPS)
    return center * inverse, inverse


def layer_norm(values, gain, offset):
    return (norm_parts(values)[0] * gain + offset).astype(BF)


def norm_back(values, gain, grad):
    hat, inverse = norm_parts(values)
    scaled = grad * gain
    back = inverse * (
        scaled
        - jnp.mean(scaled, -1, keepdims=True)
        - hat * jnp.mean(scaled * hat, -1, keepdims=True)
    )
    lead = tuple(range(values.ndim - 1))
    return back, jnp.sum(grad * hat, lead), jnp.sum(grad, lead)


def layer(shape, args):
    chips, tops, lows = shape["chip"], shape["hi"], shape["lo"]
    (
        image_rows,
        text_rows,
        segment_ids,
        cotangent,
        query_weight,
        key_weight,
        value_weight,
        attn_output,
        cross_query,
        cross_key,
        cross_value,
        cross_output,
        hidden_in,
        hidden_out,
        *norms,
    ) = args
    images, rows, width = image_rows.shape
    texts = text_rows.shape[1]
    half_rows = rows // 2
    length = rows * lows * tops
    shard = query_weight.shape[0]
    chip, core = lax.axis_index("chip"), lax.axis_index("core")
    top = lax.axis_index("hi")
    own_slot = core * images + top % images

    def swap(value):
        return lax.ppermute(value, "core", [(0, 1), (1, 0)])

    def across(value, bit):
        return lax.ppermute(value, "chip", [(i, i ^ bit) for i in range(chips)])

    def shift(value, step):
        return lax.ppermute(value, "hi", [((i + step) % tops, i) for i in range(tops)])

    def matching(number, back):
        pairs = []
        for source_core in range(2):
            for source_top in range(tops):
                slot = source_top ^ number
                target = (slot // images) * tops + source_core * images + slot % images
                source = source_core * tops + source_top
                pairs.append((target, source) if back else (source, target))
        return pairs

    def to_image(piece_of):
        got = [
            lax.ppermute(piece_of(top ^ number), ("core", "hi"), matching(number, False))
            for number in range(tops)
        ]
        whole = jnp.stack(got)
        return jnp.stack(
            [lax.dynamic_index_in_dim(whole, own_slot ^ place, 0, False) for place in range(tops)]
        )

    def from_image(pieces):
        return [
            lax.ppermute(
                lax.dynamic_index_in_dim(pieces, own_slot ^ number, 0, False),
                ("core", "hi"),
                matching(number, True),
            )
            for number in range(tops)
        ]

    def image_piece(value):
        def piece(slot):
            return lax.dynamic_slice(
                value,
                (slot % images, (slot // images) * half_rows, 0),
                (1, half_rows, width),
            )[0]

        return piece

    def to_rows(pieces):
        got = jnp.stack(from_image(pieces))
        ordered = jnp.stack(
            [lax.dynamic_index_in_dim(got, top ^ slot, 0, False) for slot in range(tops)]
        )
        ordered = ordered.reshape(2, images, half_rows, width)
        return jnp.swapaxes(ordered, 0, 1).reshape(images, rows, width)

    def tp_gather(mine):
        if lows == 1:
            other = swap(mine)
            first = jnp.where(core == 0, mine, other)
            second = jnp.where(core == 0, other, mine)
            return jnp.stack([first, second], 1).reshape(length, width)
        every = lax.all_gather(mine, ("lo", "core"))
        every = every.reshape(lows * 2, tops, half_rows, width)
        return jnp.swapaxes(every, 0, 1).reshape(length, width)

    def tp_reduce(partial):
        if lows == 1:
            cut = partial.reshape(tops, 2, half_rows, width)
            sent = lax.dynamic_index_in_dim(cut, 1 - core, 1, False).astype(BF)
            kept = lax.dynamic_index_in_dim(cut, core, 1, False)
            return kept + swap(sent).astype(F32)
        cut = jnp.swapaxes(partial.astype(BF).reshape(tops, lows * 2, half_rows, width), 0, 1)
        cut = lax.psum_scatter(cut, ("lo", "core"), scatter_dimension=0, tiled=False)
        return cut.astype(F32)

    def core_half(weight, which):
        columns = weight.shape[1] // 2
        return lax.dynamic_slice_in_dim(weight, which * columns, columns, 1)

    def pack(which):
        feeds = [core_half(weight, which) for weight in (hidden_in, hidden_out)]
        cuts = feeds[0].shape[1] // 2
        groups = [
            [core_half(w, which) for w in (query_weight, key_weight, value_weight, attn_output)],
            [core_half(w, which) for w in (cross_query, cross_key, cross_value, cross_output)],
            [w[:, :cuts] for w in feeds],
            [w[:, cuts:] for w in feeds],
        ]
        return jnp.concatenate([w for group in groups for w in group], 1)

    kept = pack(core)
    taken = swap(pack(1 - core))
    own = jnp.concatenate(
        [jnp.where(core == 0, kept, taken), jnp.where(core == 0, taken, kept)], 0
    )
    block_rows = 2 * shard
    group_width = own.shape[1] // 4

    def plane_gather(piece):
        if chips != 4:
            return lax.all_gather(piece, "chip", axis=0, tiled=True)
        side = across(piece, 1)
        over = across(piece, 2)
        corner_low = across(side[:shard], 2)
        corner_high = across(over[shard:], 1)
        corner = jnp.concatenate([corner_low, corner_high], 0)
        pieces = jnp.stack([piece, side, over, corner])
        ordered = [lax.dynamic_index_in_dim(pieces, chip ^ place, 0, False) for place in range(4)]
        return jnp.concatenate(ordered, 0)

    def plane_scatter(grads):
        if chips != 4:
            return lax.psum_scatter(grads, "chip", scatter_dimension=0, tiled=True).astype(F32)

        def rows_of(place, low, count):
            return lax.dynamic_slice_in_dim(grads, (chip ^ place) * block_rows + low, count, 0)

        by_side = across(rows_of(3, 0, shard), 1)
        by_over = across(rows_of(3, shard, shard), 2)
        to_over = jnp.concatenate(
            [rows_of(2, 0, shard).astype(F32) + by_side.astype(F32), rows_of(2, shard, shard).astype(F32)], 0
        ).astype(BF)
        to_side = jnp.concatenate(
            [rows_of(1, 0, shard).astype(F32), rows_of(1, shard, shard).astype(F32) + by_over.astype(F32)], 0
        ).astype(BF)
        over, side = across(to_over, 2), across(to_side, 1)
        return rows_of(0, 0, block_rows).astype(F32) + over.astype(F32) + side.astype(F32)

    def top_scatter(pieces):
        total = pieces[0].astype(F32)
        for step in range(1, tops):
            total = total + shift(pieces[step].astype(BF), tops - step).astype(F32)
        return total

    def core_split(total):
        cut = total.reshape(2, shard, total.shape[1])
        mine = lax.dynamic_index_in_dim(cut, core, 0, False)
        other = swap(lax.dynamic_index_in_dim(cut, 1 - core, 0, False).astype(BF)).astype(F32)
        return jnp.where(core == 0, mine, other), jnp.where(core == 0, other, mine)

    own_wide = plane_gather(own)

    def fetch(group, count):
        part = own[:, group * group_width : (group + 1) * group_width]
        columns = group_width // count
        got = [shift(part, step).reshape(block_rows, count, 1, columns) for step in range(1, tops)]
        rest = jnp.concatenate(got, 2).reshape(block_rows, (tops - 1) * group_width)
        rest = plane_gather(rest).reshape(width, count, (tops - 1) * columns)
        near = own_wide[:, group * group_width : (group + 1) * group_width]
        near = near.reshape(width, count, columns)
        return [
            jnp.concatenate([near[:, one], rest[:, one]], 1) for one in range(count)
        ]

    def give(grads):
        count = len(grads)
        columns = grads[0].shape[1] // tops
        summed = plane_scatter(jnp.concatenate(grads, 1)).reshape(block_rows, count, tops, columns)
        pieces = [summed[:, :, step].reshape(block_rows, count * columns) for step in range(tops)]
        low, high = core_split(top_scatter(pieces))
        low, high = low.reshape(shard, count, columns), high.reshape(shard, count, columns)
        return [(low[:, one], high[:, one]) for one in range(count)]

    packed_norms = lax.all_gather(jnp.stack(norms), ("chip", "core"), axis=1, tiled=True)
    gain_one, bias_one, gain_two, bias_two, gain_three, bias_three = packed_norms

    w_query, w_key, w_value, w_out = fetch(0, 4)
    inputs = to_image(image_piece(image_rows)).astype(F32)
    c_query, c_key, c_value, c_out = fetch(1, 4)
    in_low, out_low = fetch(2, 2)
    in_high, out_high = fetch(3, 2)

    text = to_image(lambda slot: text_rows[slot % images])
    if lows > 1:
        text = lax.all_gather(text, "lo", axis=1)
    text = text.reshape(tops * lows * texts, width)
    other_ids = swap(segment_ids)
    ids = jnp.where(core == top // images, segment_ids, other_ids)
    ids = lax.dynamic_index_in_dim(ids, top % images, 0, False)
    captions = jnp.repeat(ids, length // ids.shape[0])[None, :]
    ids = ids[:, None]
    cot = to_image(image_piece(cotangent))

    full_one = tp_gather(layer_norm(inputs, gain_one, bias_one))
    packed = dot(full_one, jnp.concatenate([w_query, w_key, w_value], 1)).astype(BF)
    self_mix, self_lse = self_forward(packed)
    after_attn = inputs + tp_reduce(dot(self_mix, w_out, NT))
    full_two = tp_gather(layer_norm(after_attn, gain_two, bias_two))
    queries = dot(full_two, c_query).astype(BF)
    w_text = jnp.concatenate([c_key, c_value], 1)
    keys = dot(text, w_text).astype(BF)
    cross_mix, cross_lse = cross_forward(queries, keys, ids, captions)
    after_cross = after_attn + tp_reduce(dot(cross_mix, c_out, NT))
    full_three = tp_gather(layer_norm(after_cross, gain_three, bias_three))
    full_cot = tp_gather(cot)
    gin_low, gout_low, *sums = feed(full_three, full_cot, in_low, out_low, None)
    gin_high, gout_high, out_sum, back_sum = feed(full_three, full_cot, in_high, out_high, sums)
    low_grads = give([gin_low, gout_low])
    high_grads = give([gin_high, gout_high])
    result = to_rows((after_cross + tp_reduce(out_sum)).astype(BF))

    back_three, dgain_three, dbias_three = norm_back(after_cross, gain_three, tp_reduce(back_sum))
    grad_cross = cot.astype(F32) + back_three
    full_grad = tp_gather(grad_cross.astype(BF))
    mix_grad = dot(full_grad, c_out).astype(BF)
    dq, dk, dv = cross_backward(queries, keys, cross_mix, mix_grad, cross_lse, ids, captions)
    back_sum = dot(dq, c_query, NT)
    dkv = jnp.concatenate([dk, dv], 1)
    cross_grads = give(
        [
            dot(full_two, dq, TN).astype(BF),
            dot(text, dk, TN).astype(BF),
            dot(text, dv, TN).astype(BF),
            dot(full_grad, cross_mix, TN).astype(BF),
        ]
    )
    text_part = dot(dkv, w_text, NT).astype(BF).reshape(tops, lows, texts, width)
    if lows > 1:
        text_part = lax.psum_scatter(text_part, "lo", scatter_dimension=1, tiled=True)
    got = [part.astype(F32) for part in from_image(text_part[:, 0])]
    got = jnp.stack(got)
    got = [lax.dynamic_index_in_dim(got, top ^ slot, 0, False) for slot in range(tops)]
    text_grad = jnp.stack([got[i] + got[images + i] for i in range(images)])

    back_two, dgain_two, dbias_two = norm_back(after_attn, gain_two, tp_reduce(back_sum))
    grad_attn = grad_cross + back_two
    full_grad = tp_gather(grad_attn.astype(BF))
    mix_grad = dot(full_grad, w_out).astype(BF)
    dq, dk, dv = self_backward(packed, self_mix, mix_grad, self_lse)
    dqkv = jnp.concatenate([dq, dk, dv], 1)
    dwqkv = dot(full_one, dqkv, TN).astype(BF)
    span = dq.shape[1]
    self_grads = give(
        [
            dwqkv[:, :span],
            dwqkv[:, span : 2 * span],
            dwqkv[:, 2 * span :],
            dot(full_grad, self_mix, TN).astype(BF),
        ]
    )
    back_sum = dot(dqkv, jnp.concatenate([w_query, w_key, w_value], 1), NT)
    back_one, dgain_one, dbias_one = norm_back(inputs, gain_one, tp_reduce(back_sum))
    input_grad = to_rows((grad_attn + back_one).astype(BF)).astype(F32)

    norm_sums = lax.psum(
        jnp.stack([dgain_one, dbias_one, dgain_two, dbias_two, dgain_three, dbias_three]),
        ("chip", "core", "hi", "lo"),
    )
    norm_sums = lax.dynamic_slice_in_dim(norm_sums, (chip * 2 + core) * shard, shard, 1)

    feeds = [
        jnp.concatenate([low_grads[i][0], high_grads[i][0], low_grads[i][1], high_grads[i][1]], 1)
        for i in range(2)
    ]
    joined = [jnp.concatenate(pair, 1) for pair in (*self_grads, *cross_grads)]
    return (result, input_grad, text_grad, *joined, *feeds, *[norm_sums[i] for i in range(6)])


def solution(mesh):
    fsdp, tensor = mesh.shape["fsdp"], mesh.shape["tensor"]

    def run(*args):
        images = args[0].shape[0] // fsdp
        tops = 2 * images
        shape = {"chip": fsdp // 2, "core": 2, "hi": tops, "lo": tensor // tops}
        fine = Mesh(mesh.devices.reshape(tuple(shape.values())), tuple(shape))
        first, second = ("chip", "core"), ("hi", "lo")
        wide, weight, norm = P(first, second, None), P(first, second), P(first)
        outs = (wide,) * 3 + (weight,) * 10 + (norm,) * 6
        return jax.shard_map(
            lambda *local: layer(shape, local),
            mesh=fine,
            in_specs=(wide, wide, P(first, None), wide) + (weight,) * 10 + (norm,) * 6,
            out_specs=outs,
            check_vma=False,
        )(*args)

    return run
```

time: 1800 us -> 902 us (0.50)
  waiting for transfers between devices: 993 us -> 257 us
  matrix products: 226 us -> 40.6 us
  blocking collectives: 189 us -> 49.4 us
  starting transfers between devices: 2.72 us -> 125 us
  Pallas kernels: 0 us -> 103 us
  local copies, waits for them, and re-layouts: 246 us -> 202 us
  other arithmetic: 87.7 us -> 110 us
    reduce_scatter x14 -> x0, waiting for transfers between devices: 631 us -> none  [the longest x3 222 us: grad_sum(): lax.psum_scatter(partial_sum.astype(jnp.bfloat16), 'tensor', scatter_dime...]
    all_gather x8 -> x0, waiting for transfers between devices: 359 us -> none  [the longest x3 200 us: spread_grads(): return lax.all_gather(grads_in, 'tensor', axis=1, tiled=True)]
    ppermute x0 -> x102, waiting for transfers between devices: none -> 257 us  [the longest x36 116 us: across(): return lax.ppermute(value, 'chip', [(i, i ^ bit) for i in range(chips)])]
    dot_general x86 -> x16, matrix products: 226 us -> 40.6 us  [dot(): return lax.dot_general(left, right, dims, preferred_element_type=F32)]
    dynamic_update_slice x48 -> x0, local copies, waits for them, and re-layouts: 155 us -> none  [the longest x32 143 us: attend_image(): lax.map(one_block, (grouped, jnp.arange(block_count, dtype=jnp.int32)))]
    all_gather x15 -> x1, blocking collectives: 154 us -> 8.84 us  [layer(): lax.all_gather(jnp.stack(norms), ('chip', 'core'), axis=1, tiled=True)]
    ppermute x0 -> x102, starting transfers between devices: none -> 125 us  [the longest x24 29.2 us: shift(): lax.ppermute(value, 'hi', [((i + step) % tops, i) for i in range(tops)])]
    pallas_call x0 -> x6, Pallas kernels: none -> 103 us  [the longest x2 52.1 us: feed(): pl.pallas_call(body, grid=(units // block,), in_specs=specs, out_specs=[c...]
  transfers between devices with their start and end apart: 25 -> 102, of which waited for: 20 -> 42; matrix products, arithmetic and copies ran while one was open for 14% -> 29% of each run, Pallas kernels for 0% -> 2%
where the time goes in v1:
time: 902 us; the launch traced here: 890 us
  waiting for transfers between devices  257 us (28%)
  local copies, waits for them, and re-layouts  202 us (22%)
  starting transfers between devices  125 us (14%)
  other arithmetic  110 us (12%)
  Pallas kernels  103 us (11%)
  blocking collectives  49.4 us (5%)
  matrix products  40.6 us (5%)
    ppermute x36, waiting for transfers between devices, across(): return lax.ppermute(value, 'chip', [(i, i ^ bit) for i in range(chips)])  116 us
    ppermute x24, waiting for transfers between devices, shift(): lax.ppermute(value, 'hi', [((i + step) % tops, i) for i in range(tops)])  106 us
    unnamed x316, local copies, waits for them, and re-layouts  55.9 us
    pallas_call x2, Pallas kernels, feed(): pl.pallas_call(body, grid=(units // block,), in_specs=specs, out_specs=[c...  52.1 us
    dot_general x16, matrix products, dot(): return lax.dot_general(left, right, dims, preferred_element_type=F32)  40.6 us
    psum x1, blocking collectives, layer(): lax.psum(jnp.stack([dgain_one, dbias_one, dgain_two, dbias_two, dgain_thr...  40.5 us
    ppermute x24, starting transfers between devices, shift(): lax.ppermute(value, 'hi', [((i + step) % tops, i) for i in range(tops)])  29.2 us
    ppermute x36, starting transfers between devices, across(): return lax.ppermute(value, 'chip', [(i, i ^ bit) for i in range(chips)])  28 us
  transfers between devices with their start and end apart: 102, of which 42 were waited for; matrix products, arithmetic and copies ran while one was open for 29% of the time, Pallas kernels for 2%

profile of v1, /device:TPU:9, one launch (start us, length us, event | category | flops | bytes accessed | tf_op | source)
XLA Modules:
  0.0 889.9 jit_solution(16663224332493167710)
XLA Ops:
  23.5 8.8 all_gather.3
  48.3 9.3 %collective-permute-done.34 = bf16[128,1024]{1,0:T(8,128)(2,1)S(1)} collective-permute-done((bf16[128,1024]{1,0:T(8,128)(2,1)}, bf16[128,1024]{1,0:T(8,128)(2,1)S(1)}, u32[]{:S(2)}, u32[]{:S(2)}) %collective-permute-start.34) | collective-permute-done | bytes 262176 | tf_op jit(solution)/shard_map/ppermute | solution.py:400
  68.2 8.4 collective-permute-done.47
  76.6 13.1 %collective-permute-start.4 = (bf16[4,128,1024]{2,1,0:T(8,128)(2,1)}, bf16[4,128,1024]{2,1,0:T(8,128)(2,1)}, u32[]{:S(2)}, u32[]{:S(2)}) collective-permute-start(bf16[4,128,1024]{2,1,0:T(8,128)(2,1)} %fusion.7), channel_id=1, source_target_pairs={{0,4},{4,0},{1,5},{5,1},{2,6},{6,2},{3,7},{7,3},{8,12},{12,8},{9,1... | collective-permute-start | bytes 3145736 | tf_op jit(solution)/shard_map/ppermute | solution.py:380
  91.0 8.4 collective-permute-done.12
  108.0 8.8 collective-permute-done.10
  130.5 8.8 collective-permute-done.38
  146.0 9.1 %collective-permute-done.20 = bf16[256,512]{1,0:T(8,128)(2,1)} collective-permute-done((bf16[256,512]{1,0:T(8,128)(2,1)}, bf16[256,512]{1,0:T(8,128)(2,1)}, u32[]{:S(2)}, u32[]{:S(2)}) %collective-permute-start.20) | collective-permute-done | bytes 262176 | tf_op jit(solution)/shard_map/ppermute | solution.py:386
  194.0 13.9 %collective-permute-done.14 = bf16[256,1536]{0,1:T(8,128)(2,1)} collective-permute-done((bf16[256,1536]{0,1:T(8,128)(2,1)}, bf16[256,1536]{0,1:T(8,128)(2,1)}, u32[]{:S(2)}, u32[]{:S(2)}) %collective-permute-start.14) | collective-permute-done | bytes 786464 | tf_op jit(solution)/shard_map/ppermute | solution.py:383
  215.1 9.7 %collective-permute-done.49 = bf16[256,1536]{0,1:T(8,128)(2,1)S(1)} collective-permute-done((bf16[256,1536]{0,1:T(8,128)(2,1)S(1)}, bf16[256,1536]{0,1:T(8,128)(2,1)S(1)}, u32[]{:S(2)}, u32[]{:S(2)}) %collective-permute-start.49) | collective-permute-done | bytes 786464 | tf_op jit(solution)/shard_map/ppermute | solution.py:383
  235.5 13.5 %collective-permute-done.48 = bf16[256,1536]{0,1:T(8,128)(2,1)S(1)} collective-permute-done((bf16[256,1536]{0,1:T(8,128)(2,1)S(1)}, bf16[256,1536]{0,1:T(8,128)(2,1)S(1)}, u32[]{:S(2)}, u32[]{:S(2)}) %collective-permute-start.48) | collective-permute-done | bytes 786464 | tf_op jit(solution)/shard_map/ppermute | solution.py:383
  262.5 11.9 %collective-permute-done.16 = bf16[128,1536]{0,1:T(8,128)(2,1)S(1)} collective-permute-done((bf16[128,1536]{0,1:T(8,128)(2,1)S(1)}, bf16[128,1536]{0,1:T(8,128)(2,1)S(1)}, u32[]{:S(2)}, u32[]{:S(2)}) %collective-permute-start.16) | collective-permute-done | bytes 393248 | tf_op jit(solution)/shard_map/ppermute | solution.py:383
  328.9 16.3 %shard_map.339 = (bf16[1024,512]{1,0:T(8,128)(2,1)}, f32[4,2,1024]{2,1,0:T(2,128)}) custom-call(bf16[1024,1536]{1,0:T(8,128)(2,1)} %convolution_convert_fusion.1.q_ref.k_ref.v_ref, bf16[1024,1536]{1,0:T(8,128)(2,1)} %convolution_convert_fusion.1.q_ref.k_ref.v_ref, bf16[1024,1536]{1,0:T(8,128)(2,1)} %convolution_convert_fusion.1.q_ref.k_ref.v_ref), custom_call_target="tpu_custom_call" | custom-call | flops 8589934592 | bytes 4194304 | tf_op jit(solution)/shard_map/pallas_call | solution.py:200
  451.9 24.2 %shard_map.341 = (bf16[1024,1024]{1,0:T(8,128)(2,1)}, bf16[1024,1024]{1,0:T(8,128)(2,1)}, f32[1024,1024]{1,0:T(8,128)}, f32[1024,1024]{1,0:T(8,128)}) custom-call(bf16[1024,1024]{1,0:T(8,128)(2,1)} %bitcast.534, bf16[1024,1024]{1,0:T(8,128)(2,1)} %bitcast.531, bf16[1024,1024]{1,0:T(8,128)(2,1)} %pad_maximum_fusion.18.c, bf16[1024,1024]{1,0:T(8,128)(2,1)} %pad_maximum_fusion.19.d), custom_call_target="tpu_custom_call" | custom-call | flops 12884901888 | bytes 16777216 | tf_op jit(solution)/shard_map/pallas_call | solution.py:313
  476.2 27.9 %shard_map.342 = (bf16[1024,1024]{1,0:T(8,128)(2,1)}, bf16[1024,1024]{1,0:T(8,128)(2,1)}, f32[1024,1024]{1,0:T(8,128)}, f32[1024,1024]{1,0:T(8,128)}) custom-call(bf16[1024,1024]{1,0:T(8,128)(2,1)} %bitcast.535, bf16[1024,1024]{1,0:T(8,128)(2,1)} %bitcast.532, bf16[1024,1024]{1,0:T(8,128)(2,1)} %pad_maximum_fusion.16.win_ref, ...), custom_call_target="tpu_custom_call" | custom-call | flops 12884901888 | bytes 16777216 | tf_op jit(solution)/shard_map/pallas_call | solution.py:313
  514.1 9.4 %collective-permute-done.94 = bf16[128,2048]{1,0:T(8,128)(2,1)S(1)} collective-permute-done((bf16[128,2048]{1,0:T(8,128)(2,1)S(1)}, bf16[128,2048]{1,0:T(8,128)(2,1)S(1)}, u32[]{:S(2)}, u32[]{:S(2)}) %collective-permute-start.94) | collective-permute-done | bytes 524320 | tf_op jit(solution)/shard_map/ppermute | solution.py:383
  572.3 7.5 collective-permute-done.89
  607.4 11.2 %collective-permute-done.90 = bf16[256,512]{0,1:T(8,128)(2,1)} collective-permute-done((bf16[256,512]{0,1:T(8,128)(2,1)}, bf16[256,512]{0,1:T(8,128)(2,1)}, u32[]{:S(2)}, u32[]{:S(2)}) %collective-permute-start.90) | collective-permute-done | bytes 262176 | tf_op jit(solution)/shard_map/ppermute | solution.py:386
  635.2 7.9 shard_map.343
  672.4 18.0 %collective-permute-done.81 = bf16[256,2048]{0,1:T(8,128)(2,1)S(1)} collective-permute-done((bf16[256,2048]{0,1:T(8,128)(2,1)S(1)}, bf16[256,2048]{0,1:T(8,128)(2,1)S(1)}, u32[]{:S(2)}, u32[]{:S(2)}) %collective-permute-start.81) | collective-permute-done | bytes 1048608 | tf_op jit(solution)/shard_map/ppermute | solution.py:383
  711.2 11.4 %collective-permute-done.84 = bf16[256,512]{1,0:T(8,128)(2,1)} collective-permute-done((bf16[256,512]{1,0:T(8,128)(2,1)}, bf16[256,512]{1,0:T(8,128)(2,1)}, u32[]{:S(2)}, u32[]{:S(2)}) %collective-permute-start.84) | collective-permute-done | bytes 262176 | tf_op jit(solution)/shard_map/ppermute | solution.py:386
  734.4 19.4 %shard_map.344 = (bf16[1024,512]{1,0:T(8,128)(2,1)}, bf16[1024,512]{1,0:T(8,128)(2,1)}, bf16[1024,512]{1,0:T(8,128)(2,1)}) custom-call(bf16[1024,1536]{1,0:T(8,128)(2,1)} %convolution_convert_fusion.1.q_ref.k_ref.v_ref, bf16[1024,1536]{1,0:T(8,128)(2,1)} %convolution_convert_fusion.1.q_ref.k_ref.v_ref, ...), custom_call_target="tpu_custom_call" | custom-call | flops 21474836480 | bytes 8388608 | tf_op jit(solution)/shard_map/pallas_call | solution.py:222
  794.6 40.5 %psum.7 = f32[6,1024]{1,0:T(8,128)S(1)} all-reduce(f32[6,1024]{1,0:T(8,128)S(1)} %stack.385), channel_id=1, replica_groups=mesh['chip'=4,'core'=2,'hi'=4,'lo'=1] {'chip','core','hi','lo'}, use_global_device_ids=true, to_apply=%region_18.19 | all-reduce | flops 6144 | bytes 49152 | tf_op jit(solution)/shard_map/psum | solution.py:625
  866.7 11.2 %collective-permute-done.74 = bf16[256,512]{0,1:T(8,128)(2,1)} collective-permute-done((bf16[256,512]{0,1:T(8,128)(2,1)}, bf16[256,512]{0,1:T(8,128)(2,1)}, u32[]{:S(2)}, u32[]{:S(2)}) %collective-permute-start.74) | collective-permute-done | bytes 262176 | tf_op jit(solution)/shard_map/ppermute | solution.py:386
  (775 shorter events, 557.7 us)
Async XLA Ops:
  0.7 43.0 %collective-permute-start.30 = (s32[2,128]{1,0:T(2,128)}, s32[2,128]{1,0:T(2,128)}, u32[]{:S(2)}, u32[]{:S(2)}) collective-permute-start(s32[2,128]{1,0:T(2,128)} %param.22), channel_id=1, source_target_pairs={{0,4},{4,0},{1,5},{5,1},{2,6},{6,2},{3,7},{7,3},{8,12},{12,8},{9,1... | collective-permute-start | bytes 3080 | tf_op jit(solution)/shard_map/ppermute | solution.py:380
  64.7 34.8 %collective-permute-start.12 = (bf16[256,512]{1,0:T(8,128)(2,1)S(1)}, bf16[256,512]{1,0:T(8,128)(2,1)}, u32[]{:S(2)}, u32[]{:S(2)}) collective-permute-start(bf16[256,512]{1,0:T(8,128)(2,1)S(1)} %get-tuple-element.215), channel_id=1, source_target_pairs={{3,0},{0,1},{1,2},{2,3},{7,4},{4,5},{5,6},{6,7},{11,8},{8,9},{9,10... | collective-permute-start | bytes 786440 | tf_op jit(solution)/shard_map/ppermute | solution.py:386
  66.3 38.8 %collective-permute-start.11 = (bf16[256,512]{1,0:T(8,128)(2,1)S(1)}, bf16[256,512]{1,0:T(8,128)(2,1)}, u32[]{:S(2)}, u32[]{:S(2)}) collective-permute-start(bf16[256,512]{1,0:T(8,128)(2,1)S(1)} %get-tuple-element.215), channel_id=1, source_target_pairs={{2,0},{3,1},{0,2},{1,3},{6,4},{7,5},{4,6},{5,7},{10,8},{11,9},{8,1... | collective-permute-start | bytes 786440 | tf_op jit(solution)/shard_map/ppermute | solution.py:386
  68.1 48.7 %collective-permute-start.10 = (bf16[256,512]{1,0:T(8,128)(2,1)S(1)}, bf16[256,512]{1,0:T(8,128)(2,1)}, u32[]{:S(2)}, u32[]{:S(2)}) collective-permute-start(bf16[256,512]{1,0:T(8,128)(2,1)S(1)} %get-tuple-element.215), channel_id=1, source_target_pairs={{1,0},{2,1},{3,2},{0,3},{5,4},{6,5},{7,6},{4,7},{9,8},{10,9},{11,1... | collective-permute-start | bytes 786440 | tf_op jit(solution)/shard_map/ppermute | solution.py:386
  76.6 94.5 %collective-permute-start.4 = (bf16[4,128,1024]{2,1,0:T(8,128)(2,1)}, bf16[4,128,1024]{2,1,0:T(8,128)(2,1)}, u32[]{:S(2)}, u32[]{:S(2)}) collective-permute-start(bf16[4,128,1024]{2,1,0:T(8,128)(2,1)} %fusion.7), channel_id=1, source_target_pairs={{0,4},{4,0},{1,5},{5,1},{2,6},{6,2},{3,7},{7,3},{8,12},{12,8},{9,1... | collective-permute-start | bytes 3145736 | tf_op jit(solution)/shard_map/ppermute | solution.py:380
  90.9 82.5 %collective-permute-start.37 = (bf16[4,128,1024]{2,1,0:T(8,128)(2,1)}, bf16[4,128,1024]{2,1,0:T(8,128)(2,1)}, u32[]{:S(2)}, u32[]{:S(2)}) collective-permute-start(bf16[4,128,1024]{2,1,0:T(8,128)(2,1)} %pad_maximum_fusion.29), channel_id=1, source_target_pairs={{0,4},{4,0},{1,5},{5,1},{2,6},{6,2},{3,7},{7,3},{8,12},{12,8},{9,1... | collective-permute-start | bytes 3145736 | tf_op jit(solution)/shard_map/ppermute | solution.py:380
  173.4 34.5 %collective-permute-start.14 = (bf16[256,1536]{0,1:T(8,128)(2,1)}, bf16[256,1536]{0,1:T(8,128)(2,1)}, u32[]{:S(2)}, u32[]{:S(2)}) collective-permute-start(bf16[256,1536]{0,1:T(8,128)(2,1)} %bitcast.34), channel_id=1, source_target_pairs={{0,16},{8,24},{16,0},{24,8},{1,17},{9,25},{17,1},{25,9},{2,18},{10... | collective-permute-start | bytes 2359304 | tf_op jit(solution)/shard_map/ppermute | solution.py:383
  184.6 40.2 %collective-permute-start.49 = (bf16[256,1536]{0,1:T(8,128)(2,1)S(1)}, bf16[256,1536]{0,1:T(8,128)(2,1)S(1)}, u32[]{:S(2)}, u32[]{:S(2)}) collective-permute-start(bf16[256,1536]{0,1:T(8,128)(2,1)S(1)} %bitcast.497), channel_id=1, source_target_pairs={{0,16},{8,24},{16,0},{24,8},{1,17},{9,25},{17,1},{25,9},{2,18},{10... | collective-permute-start | bytes 2359304 | tf_op jit(solution)/shard_map/ppermute | solution.py:383
  191.2 58.9 %collective-permute-start.6 = (bf16[256,2048]{1,0:T(8,128)(2,1)S(1)}, bf16[256,2048]{1,0:T(8,128)(2,1)S(1)}, u32[]{:S(2)}, u32[]{:S(2)}) collective-permute-start(bf16[256,2048]{1,0:T(8,128)(2,1)S(1)} %get-tuple-element.233), channel_id=1, source_target_pairs={{0,8},{8,0},{16,24},{24,16},{1,9},{9,1},{17,25},{25,17},{2,10},{10... | collective-permute-start | bytes 3145736 | tf_op jit(solution)/shard_map/ppermute | solution.py:383
  193.0 58.4 %collective-permute-start.7 = (bf16[256,2048]{1,0:T(8,128)(2,1)S(1)}, bf16[256,2048]{1,0:T(8,128)(2,1)S(1)}, u32[]{:S(2)}, u32[]{:S(2)}) collective-permute-start(bf16[256,2048]{1,0:T(8,128)(2,1)S(1)} %get-tuple-element.233), channel_id=1, source_target_pairs={{0,16},{8,24},{16,0},{24,8},{1,17},{9,25},{17,1},{25,9},{2,18},{10... | collective-permute-start | bytes 3145736 | tf_op jit(solution)/shard_map/ppermute | solution.py:383
  207.9 41.1 %collective-permute-start.48 = (bf16[256,1536]{0,1:T(8,128)(2,1)S(1)}, bf16[256,1536]{0,1:T(8,128)(2,1)S(1)}, u32[]{:S(2)}, u32[]{:S(2)}) collective-permute-start(bf16[256,1536]{0,1:T(8,128)(2,1)S(1)} %bitcast.498), channel_id=1, source_target_pairs={{0,8},{8,0},{16,24},{24,16},{1,9},{9,1},{17,25},{25,17},{2,10},{10... | collective-permute-start | bytes 2359304 | tf_op jit(solution)/shard_map/ppermute | solution.py:383
  215.0 42.6 %collective-permute-start.44 = (bf16[128,1536]{0,1:T(8,128)(2,1)S(1)}, bf16[128,1536]{0,1:T(8,128)(2,1)S(1)}, u32[]{:S(2)}, u32[]{:S(2)}) collective-permute-start(bf16[128,1536]{0,1:T(8,128)(2,1)S(1)} %slice.433), channel_id=1, source_target_pairs={{0,8},{8,0},{16,24},{24,16},{1,9},{9,1},{17,25},{25,17},{2,10},{10... | collective-permute-start | bytes 1179656 | tf_op jit(solution)/shard_map/ppermute | solution.py:383
  249.1 35.7 %collective-permute-start.25 = (bf16[128,1536]{0,1:T(8,128)(2,1)}, bf16[128,1536]{0,1:T(8,128)(2,1)}, u32[]{:S(2)}, u32[]{:S(2)}) collective-permute-start(bf16[128,1536]{0,1:T(8,128)(2,1)} %slice.420), channel_id=1, source_target_pairs={{0,8},{8,0},{16,24},{24,16},{1,9},{9,1},{17,25},{25,17},{2,10},{10... | collective-permute-start | bytes 1179656 | tf_op jit(solution)/shard_map/ppermute | solution.py:383
  250.1 34.9 %collective-permute-start.24 = (bf16[128,1536]{0,1:T(8,128)(2,1)}, bf16[128,1536]{0,1:T(8,128)(2,1)}, u32[]{:S(2)}, u32[]{:S(2)}) collective-permute-start(bf16[128,1536]{0,1:T(8,128)(2,1)} %slice.419), channel_id=1, source_target_pairs={{0,16},{8,24},{16,0},{24,8},{1,17},{9,25},{17,1},{25,9},{2,18},{10... | collective-permute-start | bytes 1179656 | tf_op jit(solution)/shard_map/ppermute | solution.py:383
  257.7 93.6 %collective-permute-start.51 = (bf16[128,1536]{0,1:T(8,128)(2,1)}, bf16[128,1536]{0,1:T(8,128)(2,1)}, u32[]{:S(2)}, u32[]{:S(2)}) collective-permute-start(bf16[128,1536]{0,1:T(8,128)(2,1)} %slice.442), channel_id=1, source_target_pairs={{0,8},{8,0},{16,24},{24,16},{1,9},{9,1},{17,25},{25,17},{2,10},{10... | collective-permute-start | bytes 1179656 | tf_op jit(solution)/shard_map/ppermute | solution.py:383
  274.4 76.8 %collective-permute-start.50 = (bf16[128,1536]{0,1:T(8,128)(2,1)}, bf16[128,1536]{0,1:T(8,128)(2,1)}, u32[]{:S(2)}, u32[]{:S(2)}) collective-permute-start(bf16[128,1536]{0,1:T(8,128)(2,1)} %slice.441), channel_id=1, source_target_pairs={{0,16},{8,24},{16,0},{24,8},{1,17},{9,25},{17,1},{25,9},{2,18},{10... | collective-permute-start | bytes 1179656 | tf_op jit(solution)/shard_map/ppermute | solution.py:383
  524.3 36.3 %collective-permute-start.97 = (bf16[256,2048]{1,0:T(8,128)(2,1)S(1)}, bf16[256,2048]{1,0:T(8,128)(2,1)S(1)}, u32[]{:S(2)}, u32[]{:S(2)}) collective-permute-start(bf16[256,2048]{1,0:T(8,128)(2,1)S(1)} %pad_maximum_fusion.41), channel_id=1, source_target_pairs={{0,8},{8,0},{16,24},{24,16},{1,9},{9,1},{17,25},{25,17},{2,10},{10... | collective-permute-start | bytes 3145736 | tf_op jit(solution)/shard_map/ppermute | solution.py:383
  525.7 34.9 %collective-permute-start.95 = (bf16[256,2048]{1,0:T(8,128)(2,1)S(1)}, bf16[256,2048]{1,0:T(8,128)(2,1)S(1)}, u32[]{:S(2)}, u32[]{:S(2)}) collective-permute-start(bf16[256,2048]{1,0:T(8,128)(2,1)S(1)} %pad_maximum_fusion.40), channel_id=1, source_target_pairs={{0,16},{8,24},{16,0},{24,8},{1,17},{9,25},{17,1},{25,9},{2,18},{10... | collective-permute-start | bytes 3145736 | tf_op jit(solution)/shard_map/ppermute | solution.py:383
  558.8 68.7 %collective-permute-start.58 = (bf16[4,128,1024]{2,1,0:T(8,128)(2,1)}, bf16[4,128,1024]{2,1,0:T(8,128)(2,1)}, u32[]{:S(2)}, u32[]{:S(2)}) collective-permute-start(bf16[4,128,1024]{2,1,0:T(8,128)(2,1)} %get-tuple-element.174), channel_id=1, source_target_pairs={{0,4},{4,0},{1,5},{5,1},{2,6},{6,2},{3,7},{7,3},{8,12},{12,8},{9,1... | collective-permute-start | bytes 3145736 | tf_op jit(solution)/shard_map/ppermute | solution.py:380
  776.8 69.8 %collective-permute-start.73 = (bf16[256,2048]{1,0:T(8,128)(2,1)}, bf16[256,2048]{1,0:T(8,128)(2,1)}, u32[]{:S(2)}, u32[]{:S(2)}) collective-permute-start(bf16[256,2048]{1,0:T(8,128)(2,1)} %pad_maximum_fusion.35), channel_id=1, source_target_pairs={{0,8},{8,0},{16,24},{24,16},{1,9},{9,1},{17,25},{25,17},{2,10},{10... | collective-permute-start | bytes 3145736 | tf_op jit(solution)/shard_map/ppermute | solution.py:383
  778.2 68.4 %collective-permute-start.71 = (bf16[256,2048]{1,0:T(8,128)(2,1)}, bf16[256,2048]{1,0:T(8,128)(2,1)}, u32[]{:S(2)}, u32[]{:S(2)}) collective-permute-start(bf16[256,2048]{1,0:T(8,128)(2,1)} %pad_maximum_fusion.34), channel_id=1, source_target_pairs={{0,16},{8,24},{16,0},{24,8},{1,17},{9,25},{17,1},{25,9},{2,18},{10... | collective-permute-start | bytes 3145736 | tf_op jit(solution)/shard_map/ppermute | solution.py:383
  783.4 51.7 %collective-permute-start.62 = (bf16[128,1024]{1,0:T(8,128)(2,1)}, bf16[128,1024]{1,0:T(8,128)(2,1)}, u32[]{:S(2)}, u32[]{:S(2)}) collective-permute-start(bf16[128,1024]{1,0:T(8,128)(2,1)} %get-tuple-element.200), channel_id=1, source_target_pairs={{0,0},{1,1},{4,2},{5,3},{2,4},{3,5},{6,6},{7,7},{8,8},{9,9},{12,10... | collective-permute-start | bytes 786440 | tf_op jit(solution)/shard_map/ppermute | solution.py:410
  790.1 48.1 %collective-permute-start.65 = (bf16[128,1024]{1,0:T(8,128)(2,1)}, bf16[128,1024]{1,0:T(8,128)(2,1)S(1)}, u32[]{:S(2)}, u32[]{:S(2)}) collective-permute-start(bf16[128,1024]{1,0:T(8,128)(2,1)} %get-tuple-element.201), channel_id=1, source_target_pairs={{5,0},{4,1},{1,2},{0,3},{7,4},{6,5},{3,6},{2,7},{13,8},{12,9},{9,1... | collective-permute-start | bytes 786440 | tf_op jit(solution)/shard_map/ppermute | solution.py:410
  790.1 48.1 %collective-permute-start.64 = (bf16[128,1024]{1,0:T(8,128)(2,1)}, bf16[128,1024]{1,0:T(8,128)(2,1)}, u32[]{:S(2)}, u32[]{:S(2)}) collective-permute-start(bf16[128,1024]{1,0:T(8,128)(2,1)} %get-tuple-element.202), channel_id=1, source_target_pairs={{4,0},{5,1},{0,2},{1,3},{6,4},{7,5},{2,6},{3,7},{12,8},{13,9},{8,1... | collective-permute-start | bytes 786440 | tf_op jit(solution)/shard_map/ppermute | solution.py:410
  (219 other events, 4625.6 us)
